TPU v7x, 256 devices: a whole 4x4x8 slice. The times are simulated.
256 devices in a mesh: gx: 16 (over x, y), gy: 8 (over z_hi, core), gz: 2 (over z_lo).
Axes of the slice: x: 4, y: 4, z: 8 (z_hi: 4, z_lo: 2; z = z_hi * 2 + z_lo), core: 2. Of those that a mesh axis runs over, the one named last changes fastest.
Arguments:
- density: float32 [8, 1024, 2048], P('gz', 'gx', 'gy'), may hold values from 0.01 to 0.05
- tap_index: int32 [8, 16, 16, 128], P('gz', 'gx', 'gy'), may hold values from 0 to 8191
- tap_current: float32 [8, 16, 16, 128], P('gz', 'gx', 'gy'), may hold values from 0.5 to 4
- pad_cond: float32 [8, 1024, 2048], P('gz', 'gx', 'gy'), may hold values from 0.05 to 0.5
- row_cond: float32 [8, 1024, 2048], P('gz', 'gx', 'gy'), may hold values from 0.5 to 1.2
- col_cond: float32 [8, 1024, 2048], P('gz', 'gx', 'gy'), may hold values from 1 to 2
- material: int32 [8, 1024, 2048], P('gz', 'gx', 'gy'), may hold values from 0 to 3
- leak_rates: float32 [4], replicated, may hold values from 0.5 to 4
- theta_start: float32 [32, 1024, 2048], P(None, 'gx', ('gy', 'gz')), may hold values from -6 to 6
- kappa: float32 [32, 1024, 2048], P(None, 'gx', ('gy', 'gz')), may hold values from 1 to 2
- inv_capacity: float32 [32, 1024, 2048], P(None, 'gx', ('gy', 'gz')), may hold values from 0.04 to 0.08
Outputs:
- ir_drop: float32 [8, 1024, 2048], P('gz', 'gx', 'gy')
- temperature: float32 [32, 1024, 2048], P(None, 'gx', ('gy', 'gz'))
All inputs are finite; a program needn't handle non-finite values.
Results may differ from a plain program's by a relative error of at most 0.00002.
Values sent between devices are 32-bit elements; how exact they have to be, the bound alone decides.
A program may use at most 128 MiB of HBM per device.

v0:
```python
import jax
import jax.numpy as jnp
from jax import lax
from jax.sharding import PartitionSpec as P

LAYERS_TIER = 4
MATERIALS = 4
SWEEPS = 16
STEPS = 4
TX = 64
TY = 128


def from_behind(block, axis, distance):
    devices = range(lax.axis_size(axis))
    route = [(i - distance, i) for i in devices if i - distance in devices]
    return lax.ppermute(block, axis, route)


def with_halo(cells, sides, width):
    for axis, dim in sides:
        count = lax.axis_size(axis)
        ends = count - 1
        head = lax.slice_in_dim(cells, 0, width, axis=dim)
        tail = lax.slice_in_dim(cells, cells.shape[dim] - width, cells.shape[dim], axis=dim)
        cells = jnp.concatenate(
            [
                lax.ppermute(tail, axis, [(i, (i + 1) % count) for i in range(ends)]),
                cells,
                lax.ppermute(head, axis, [((i + 1) % count, i) for i in range(ends)]),
            ],
            axis=dim,
        )
    return cells


def place_taps(tap_current, tap_index, tiers, rows, cols):
    blocks_x = rows // TX
    blocks_y = cols // TY
    base = (jnp.arange(tiers * blocks_x * blocks_y, dtype=jnp.int32) * (TX * TY)).reshape(
        tiers, blocks_x, blocks_y, 1
    )
    flat_index = (base + tap_index).reshape(-1)
    summed = (
        jnp.zeros((tiers * blocks_x * blocks_y * TX * TY,), jnp.float32)
        .at[flat_index]
        .add(tap_current.reshape(-1))
    )
    summed = summed.reshape(tiers, blocks_x, blocks_y, TX, TY).transpose(0, 1, 3, 2, 4)
    return summed.reshape(tiers, rows, cols)


def relax(source, gxp, gxm, gyp, gym, denom, padded):
    beside_all = gxp * padded[:, 2:, 1:-1] + gxm * padded[:, :-2, 1:-1]
    beside_all = beside_all + gyp * padded[:, 1:-1, 2:] + gym * padded[:, 1:-1, :-2]
    return (source + beside_all) / denom


def harmonic(first, second):
    return 2.0 * first * second / (first + second)


def heat_step(theta, padded, links, inv_capacity, heat):
    kxn, kxp, kyn, kyp, kzu, kzd = links
    zero_layer = jnp.zeros_like(theta[:1])
    upper = jnp.concatenate([theta[1:], zero_layer], 0)
    lower = jnp.concatenate([zero_layer, theta[:-1]], 0)
    flow = kxn * (padded[:, 2:, 1:-1] - theta) + kxp * (padded[:, :-2, 1:-1] - theta)
    flow = flow + kyn * (padded[:, 1:-1, 2:] - theta) + kyp * (padded[:, 1:-1, :-2] - theta)
    flow = flow + kzu * (upper - theta) + kzd * (lower - theta)
    return theta + inv_capacity * (flow + heat)


def vertical_links(kappa):
    inner = harmonic(kappa[:-1], kappa[1:])
    kzu = jnp.concatenate([inner, jnp.zeros_like(kappa[:1])], 0)
    kzd = jnp.concatenate([kappa[:1], inner], 0)
    return (kzu, kzd)


def leakage(material, leak_rates, drop):
    leak = jnp.zeros(drop.shape, jnp.float32)
    for kind in range(MATERIALS):
        leak = leak + jnp.where(material == kind, leak_rates[kind], 0.0)
    return leak * jnp.exp(-drop)


def spread_heat(power_map, layers, trows, tcols):
    filler = jnp.zeros((power_map.shape[0], LAYERS_TIER - 1, trows, tcols), jnp.float32)
    return jnp.concatenate([power_map[:, None], filler], 1).reshape(layers, trows, tcols)


def shards(
    density,
    tap_index,
    tap_current,
    pad_cond,
    row_cond,
    col_cond,
    material,
    leak_rates,
    theta_start,
    kappa,
    inv_capacity,
):
    tiers_dev, rows, cols = density.shape
    source = density + place_taps(tap_current, tap_index, tiers_dev, rows, cols)
    row_pos = lax.axis_index("gx") * rows + jnp.arange(rows, dtype=jnp.int32)
    col_pos = lax.axis_index("gy") * cols + jnp.arange(cols, dtype=jnp.int32)
    gxp = jnp.where((row_pos < lax.axis_size("gx") * rows - 1)[None, :, None], row_cond, 0.0)
    gyp = jnp.where((col_pos < lax.axis_size("gy") * cols - 1)[None, None, :], col_cond, 0.0)
    drop = jnp.zeros_like(source)
    below = from_behind(gxp[:, -1:, :], "gx", 1)
    left = from_behind(gyp[:, :, -1:], "gy", 1)
    gxm = jnp.concatenate([below, gxp[:, :-1]], 1)
    gym = jnp.concatenate([left, gyp[:, :, :-1]], 2)
    denom = pad_cond + gxp + gxm + gyp + gym

    def sweep(count, state):
        padded = with_halo(state, (("gx", 1), ("gy", 2)), 1)
        return relax(source, gxp, gxm, gyp, gym, denom, padded)

    drop = lax.fori_loop(0, SWEEPS, sweep, drop)
    after_row = from_behind(drop[:, :1, :], "gx", -1)
    after_col = from_behind(drop[:, :, :1], "gy", -1)
    row_diff = jnp.concatenate([drop[:, 1:], after_row], 1) - drop
    col_diff = jnp.concatenate([drop[:, :, 1:], after_col], 2) - drop
    power = pad_cond * drop * drop + gxp * row_diff * row_diff + gyp * col_diff * col_diff
    power = power + leakage(material, leak_rates, drop)
    relayed = lax.all_to_all(power, "gz", split_axis=2, concat_axis=0, tiled=True)
    layers, trows, tcols = theta_start.shape
    theta = theta_start
    heat = spread_heat(relayed, layers, trows, tcols)
    kpad = with_halo(kappa, (("gx", 1), (("gy", "gz"), 2)), 1)
    kzu, kzd = vertical_links(kappa)
    links = (
        harmonic(kappa, kpad[:, 2:, 1:-1]),
        harmonic(kappa, kpad[:, :-2, 1:-1]),
        harmonic(kappa, kpad[:, 1:-1, 2:]),
        harmonic(kappa, kpad[:, 1:-1, :-2]),
        kzu,
        kzd,
    )
    for step in range(STEPS):
        padded = with_halo(theta, (("gx", 1), (("gy", "gz"), 2)), 1)
        theta = heat_step(theta, padded, links, inv_capacity, heat)
    return (drop, theta)


def solution(mesh):
    return jax.shard_map(
        shards,
        mesh=mesh,
        in_specs=(
            P("gz", "gx", "gy"),
            P("gz", "gx", "gy", None),
            P("gz", "gx", "gy", None),
            P("gz", "gx", "gy"),
            P("gz", "gx", "gy"),
            P("gz", "gx", "gy"),
            P("gz", "gx", "gy"),
            P(),
            P(None, "gx", ("gy", "gz")),
            P(None, "gx", ("gy", "gz")),
            P(None, "gx", ("gy", "gz")),
        ),
        out_specs=(P("gz", "gx", "gy"), P(None, "gx", ("gy", "gz"))),
        check_vma=False,
    )
```

profile of v0, /device:TPU:103, one launch (start us, length us, event | category | flops | bytes accessed | tf_op | source)
XLA Modules:
  0.0 594.9 jit_solution(4267225537166141164)
XLA Ops:
  13.3 6.3 %collective-permute-start.5 = (f32[4,64,1]{2,1,0:T(8,128)S(1)}, f32[4,64,1]{2,1,0:T(8,128)S(1)}, u32[]{:S(2)}, u32[]{:S(2)}) collective-permute-start(f32[4,64,1]{2,1,0:T(8,128)S(1)} %slice.314), channel_id=1, source_target_pairs={{0,2},{2,4},{4,6},{6,8},{8,10},{10,12},{12,14},{1,3},{3,5},{5,7},{... | collective-permute-start | bytes 3080 | tf_op jit(solution)/shard_map/ppermute | solution.py:17
  22.1 6.2 %scatter_custom_fusion = f32[65536]{0:T(1024)S(1)} fusion(s32[1024]{0:T(1024)S(1)} %bitcast.36, f32[1024]{0:T(1024)} %bitcast.37, f32[]{:T(128)} %constant.21.clone.1), kind=kCustom, calls=%fused_computation.141 | custom fusion | flops 1024 | bytes 262656 | tf_op jit(solution)/shard_map/scatter-add | solution.py:47
  28.7 5.5 collective-permute-start.6
  34.4 329.9 %while.11 = (s32[]{:T(128)}, f32[4,64,256]{2,1,0:T(8,128)S(1)}, f32[4,64,256]{2,1,0:T(8,128)S(1)}, f32[4,64,256]{2,1,0:T(8,128)S(1)}, f32[4,64,256]{2,1,0:T(8,12...) while((s32[]{:T(128)}, f32[4,64,256]{2,1,0:T(8,128)S(1)}, ...), condition=%wide.region_2.3_spmd.clone, body=%wide.region_1.2_spmd.clone.sunk | while | flops 1314819 | bytes 3234511 | solution.py:123
  50.5 7.5 %collective-permute-done.3 = f32[4,66,1]{2,1,0:T(8,128)S(1)} collective-permute-done((f32[4,66,1]{2,1,0:T(8,128)S(1)}, f32[4,66,1]{2,1,0:T(8,128)S(1)}, u32[]{:S(2)}, u32[]{:S(2)}) %collective-permute-start.3) | collective-permute-done | bytes 1088 | tf_op jit(solution)/shard_map/while/body/eval_jaxpr/ppermute | solution.py:30
  71.3 7.8 %collective-permute-done.3 = f32[4,66,1]{2,1,0:T(8,128)S(1)} collective-permute-done((f32[4,66,1]{2,1,0:T(8,128)S(1)}, f32[4,66,1]{2,1,0:T(8,128)S(1)}, u32[]{:S(2)}, u32[]{:S(2)}) %collective-permute-start.3) | collective-permute-done | bytes 1088 | tf_op jit(solution)/shard_map/while/body/eval_jaxpr/ppermute | solution.py:30
  92.8 6.6 %collective-permute-done.3 = f32[4,66,1]{2,1,0:T(8,128)S(1)} collective-permute-done((f32[4,66,1]{2,1,0:T(8,128)S(1)}, f32[4,66,1]{2,1,0:T(8,128)S(1)}, u32[]{:S(2)}, u32[]{:S(2)}) %collective-permute-start.3) | collective-permute-done | bytes 1088 | tf_op jit(solution)/shard_map/while/body/eval_jaxpr/ppermute | solution.py:30
  113.2 6.5 %collective-permute-done.3 = f32[4,66,1]{2,1,0:T(8,128)S(1)} collective-permute-done((f32[4,66,1]{2,1,0:T(8,128)S(1)}, f32[4,66,1]{2,1,0:T(8,128)S(1)}, u32[]{:S(2)}, u32[]{:S(2)}) %collective-permute-start.3) | collective-permute-done | bytes 1088 | tf_op jit(solution)/shard_map/while/body/eval_jaxpr/ppermute | solution.py:30
  133.6 6.5 %collective-permute-done.3 = f32[4,66,1]{2,1,0:T(8,128)S(1)} collective-permute-done((f32[4,66,1]{2,1,0:T(8,128)S(1)}, f32[4,66,1]{2,1,0:T(8,128)S(1)}, u32[]{:S(2)}, u32[]{:S(2)}) %collective-permute-start.3) | collective-permute-done | bytes 1088 | tf_op jit(solution)/shard_map/while/body/eval_jaxpr/ppermute | solution.py:30
  153.9 6.5 %collective-permute-done.3 = f32[4,66,1]{2,1,0:T(8,128)S(1)} collective-permute-done((f32[4,66,1]{2,1,0:T(8,128)S(1)}, f32[4,66,1]{2,1,0:T(8,128)S(1)}, u32[]{:S(2)}, u32[]{:S(2)}) %collective-permute-start.3) | collective-permute-done | bytes 1088 | tf_op jit(solution)/shard_map/while/body/eval_jaxpr/ppermute | solution.py:30
  174.3 6.5 %collective-permute-done.3 = f32[4,66,1]{2,1,0:T(8,128)S(1)} collective-permute-done((f32[4,66,1]{2,1,0:T(8,128)S(1)}, f32[4,66,1]{2,1,0:T(8,128)S(1)}, u32[]{:S(2)}, u32[]{:S(2)}) %collective-permute-start.3) | collective-permute-done | bytes 1088 | tf_op jit(solution)/shard_map/while/body/eval_jaxpr/ppermute | solution.py:30
  194.7 6.5 %collective-permute-done.3 = f32[4,66,1]{2,1,0:T(8,128)S(1)} collective-permute-done((f32[4,66,1]{2,1,0:T(8,128)S(1)}, f32[4,66,1]{2,1,0:T(8,128)S(1)}, u32[]{:S(2)}, u32[]{:S(2)}) %collective-permute-start.3) | collective-permute-done | bytes 1088 | tf_op jit(solution)/shard_map/while/body/eval_jaxpr/ppermute | solution.py:30
  215.0 6.5 %collective-permute-done.3 = f32[4,66,1]{2,1,0:T(8,128)S(1)} collective-permute-done((f32[4,66,1]{2,1,0:T(8,128)S(1)}, f32[4,66,1]{2,1,0:T(8,128)S(1)}, u32[]{:S(2)}, u32[]{:S(2)}) %collective-permute-start.3) | collective-permute-done | bytes 1088 | tf_op jit(solution)/shard_map/while/body/eval_jaxpr/ppermute | solution.py:30
  235.4 6.5 %collective-permute-done.3 = f32[4,66,1]{2,1,0:T(8,128)S(1)} collective-permute-done((f32[4,66,1]{2,1,0:T(8,128)S(1)}, f32[4,66,1]{2,1,0:T(8,128)S(1)}, u32[]{:S(2)}, u32[]{:S(2)}) %collective-permute-start.3) | collective-permute-done | bytes 1088 | tf_op jit(solution)/shard_map/while/body/eval_jaxpr/ppermute | solution.py:30
  255.7 6.5 %collective-permute-done.3 = f32[4,66,1]{2,1,0:T(8,128)S(1)} collective-permute-done((f32[4,66,1]{2,1,0:T(8,128)S(1)}, f32[4,66,1]{2,1,0:T(8,128)S(1)}, u32[]{:S(2)}, u32[]{:S(2)}) %collective-permute-start.3) | collective-permute-done | bytes 1088 | tf_op jit(solution)/shard_map/while/body/eval_jaxpr/ppermute | solution.py:30
  276.1 6.5 %collective-permute-done.3 = f32[4,66,1]{2,1,0:T(8,128)S(1)} collective-permute-done((f32[4,66,1]{2,1,0:T(8,128)S(1)}, f32[4,66,1]{2,1,0:T(8,128)S(1)}, u32[]{:S(2)}, u32[]{:S(2)}) %collective-permute-start.3) | collective-permute-done | bytes 1088 | tf_op jit(solution)/shard_map/while/body/eval_jaxpr/ppermute | solution.py:30
  296.5 6.5 %collective-permute-done.3 = f32[4,66,1]{2,1,0:T(8,128)S(1)} collective-permute-done((f32[4,66,1]{2,1,0:T(8,128)S(1)}, f32[4,66,1]{2,1,0:T(8,128)S(1)}, u32[]{:S(2)}, u32[]{:S(2)}) %collective-permute-start.3) | collective-permute-done | bytes 1088 | tf_op jit(solution)/shard_map/while/body/eval_jaxpr/ppermute | solution.py:30
  316.8 6.5 %collective-permute-done.3 = f32[4,66,1]{2,1,0:T(8,128)S(1)} collective-permute-done((f32[4,66,1]{2,1,0:T(8,128)S(1)}, f32[4,66,1]{2,1,0:T(8,128)S(1)}, u32[]{:S(2)}, u32[]{:S(2)}) %collective-permute-start.3) | collective-permute-done | bytes 1088 | tf_op jit(solution)/shard_map/while/body/eval_jaxpr/ppermute | solution.py:30
  337.2 6.5 %collective-permute-done.3 = f32[4,66,1]{2,1,0:T(8,128)S(1)} collective-permute-done((f32[4,66,1]{2,1,0:T(8,128)S(1)}, f32[4,66,1]{2,1,0:T(8,128)S(1)}, u32[]{:S(2)}, u32[]{:S(2)}) %collective-permute-start.3) | collective-permute-done | bytes 1088 | tf_op jit(solution)/shard_map/while/body/eval_jaxpr/ppermute | solution.py:30
  357.6 6.5 %collective-permute-done.3 = f32[4,66,1]{2,1,0:T(8,128)S(1)} collective-permute-done((f32[4,66,1]{2,1,0:T(8,128)S(1)}, f32[4,66,1]{2,1,0:T(8,128)S(1)}, u32[]{:S(2)}, u32[]{:S(2)}) %collective-permute-start.3) | collective-permute-done | bytes 1088 | tf_op jit(solution)/shard_map/while/body/eval_jaxpr/ppermute | solution.py:30
  385.5 6.2 %all-to-all-start = ((f32[2,1,32768]{2,1,0:T(1,128)}), f32[2,1,32768]{2,1,0:T(1,128)S(1)}, u32[]{:S(2)}, u32[]{:S(2)}) async-start(f32[2,1,32768]{2,1,0:T(1,128)} %reshape.84), calls=%async_computation | async-start | bytes 524288 | tf_op jit(solution)/shard_map/all_to_all | solution.py:130
  402.3 5.3 collective-permute-start.13
  432.4 25.5 %fusion.64 = (f32[32,64,128]{1,0,2:T(8,128)S(1)}, f32[32,64,128]{1,0,2:T(8,128)}, f32[32,64,128]{1,0,2:T(8,128)}, f32[32,64,128]{1,0,2:T(8,128)}, f32[32,64,128]{1,0,2:T(8,128)}) fusion(f32[32,64,128]{1,0,2:T(8,128)S(1)} %copy-done.4, f32[32,64,128]{1,0,2:T(8,128)} %copy.192, f32[32,64,128]{1,0,2:T(8,128)S(1)} %bitcast.25, ...), kind=kLoop, calls=%fused_computation.100 | loop fusion | flops 13107200 | bytes 12616704 | tf_op jit(solution)/shard_map/add | solution.py:71
  468.1 5.5 collective-permute-start.16
  482.1 5.7 collective-permute-start.19
  490.4 12.5 %fusion.48 = f32[32,64,128]{1,0,2:T(8,128)S(1)} fusion(f32[32,64,128]{1,0,2:T(8,128)S(1)} %get-tuple-element.110, f32[32,64,128]{1,0,2:T(8,128)S(1)} %copy-done.9, f32[32,64,128]{1,0,2:T(8,128)} %bitcast.26, f32[32,64,128]{1,0,2:T(8,128)} %get-tuple-element.114, f32[32,66,1]{1,0,2:T(8,128)S(1)} %collective-permute-done.19, f32[32,1,128]{1,0,2:T(8,128)} %copy.195, ...), kind=kLoop, calls=%fused_computation.76 | loop fusion | flops 7602176 | bytes 11518464 | tf_op jit(solution)/shard_map/add | solution.py:71
  510.8 5.8 collective-permute-start.20
  525.2 5.1 collective-permute-start.23
  533.0 12.4 %fusion.32 = f32[32,64,128]{1,0,2:T(8,128)S(1)} fusion(f32[32,64,128]{1,0,2:T(8,128)S(1)} %copy-done.2, f32[32,64,128]{1,0,2:T(8,128)S(1)} %copy-done.10, f32[32,64,128]{1,0,2:T(8,128)} %bitcast.27, f32[32,64,128]{1,0,2:T(8,128)} %get-tuple-element.114, f32[32,66,1]{1,0,2:T(8,128)S(1)} %collective-permute-done.23, f32[32,1,128]{1,0,2:T(8,128)} %copy.202, ...), kind=kLoop, calls=%fused_computation.52 | loop fusion | flops 7602176 | bytes 11518464 | tf_op jit(solution)/shard_map/add | solution.py:71
  555.4 5.5 collective-permute-start.24
  569.3 5.4 collective-permute-start.27
  577.3 13.4 %fusion.16 = f32[32,64,128]{1,0,2:T(8,128)} fusion(f32[32,64,128]{1,0,2:T(8,128)S(1)} %fusion.32, f32[32,64,128]{1,0,2:T(8,128)S(1)} %copy-done.11, f32[32,64,128]{1,0,2:T(8,128)S(1)} %bitcast.28, f32[32,64,128]{1,0,2:T(8,128)} %get-tuple-element.114, f32[32,66,1]{1,0,2:T(8,128)S(1)} %collective-permute-done.27, f32[32,1,128]{1,0,2:T(8,128)} %copy.209, ...), kind=kLoop, calls=%fused_computation.28 | loop fusion | flops 7602176 | bytes 11518464 | tf_op jit(solution)/shard_map/add | solution.py:71
  (346 shorter events, 359.0 us)
Async XLA Ops:
  2.4 392.9 %collective-permute-start.7 = (f32[32,1,128]{2,0,1:T(8,128)}, f32[32,1,128]{2,0,1:T(8,128)}, u32[]{:S(2)}, u32[]{:S(2)}) collective-permute-start(f32[32,1,128]{2,0,1:T(8,128)} %bitcast.16), channel_id=1, source_target_pairs={{16,0},{32,16},{48,32},{64,48},{80,64},{96,80},{112,96},{128,112},... | collective-permute-start | bytes 49160 | tf_op jit(solution)/shard_map/ppermute | solution.py:30
  7.3 384.4 %collective-permute-start.9 = (f32[32,1,128]{2,0,1:T(8,128)}, f32[32,1,128]{2,0,1:T(8,128)}, u32[]{:S(2)}, u32[]{:S(2)}) collective-permute-start(f32[32,1,128]{2,0,1:T(8,128)} %bitcast.18), channel_id=1, source_target_pairs={{0,16},{16,32},{32,48},{48,64},{64,80},{80,96},{96,112},{112,128},... | collective-permute-start | bytes 49160 | tf_op jit(solution)/shard_map/ppermute | solution.py:28
  10.3 23.9 %collective-permute-start.4 = (f32[4,1,256]{2,1,0:T(1,128)S(1)}, f32[4,1,256]{2,1,0:T(1,128)S(1)}, u32[]{:S(2)}, u32[]{:S(2)}) collective-permute-start(f32[4,1,256]{2,1,0:T(1,128)S(1)} %slice.312), channel_id=1, source_target_pairs={{0,16},{16,32},{32,48},{48,64},{64,80},{80,96},{96,112},{112,128},... | collective-permute-start | bytes 12296 | tf_op jit(solution)/shard_map/ppermute | solution.py:17
  13.3 20.9 %collective-permute-start.5 = (f32[4,64,1]{2,1,0:T(8,128)S(1)}, f32[4,64,1]{2,1,0:T(8,128)S(1)}, u32[]{:S(2)}, u32[]{:S(2)}) collective-permute-start(f32[4,64,1]{2,1,0:T(8,128)S(1)} %slice.314), channel_id=1, source_target_pairs={{0,2},{2,4},{4,6},{6,8},{8,10},{10,12},{12,14},{1,3},{3,5},{5,7},{... | collective-permute-start | bytes 3080 | tf_op jit(solution)/shard_map/ppermute | solution.py:17
  28.7 382.5 %collective-permute-start.6 = (f32[32,1,128]{2,0,1:T(8,128)}, f32[32,1,128]{2,0,1:T(8,128)}, u32[]{:S(2)}, u32[]{:S(2)}) collective-permute-start(f32[32,1,128]{2,0,1:T(8,128)} %bitcast.15), channel_id=1, source_target_pairs={{16,0},{32,16},{48,32},{64,48},{80,64},{96,80},{112,96},{128,112},... | collective-permute-start | bytes 49160 | tf_op jit(solution)/shard_map/ppermute | solution.py:30
  48.4 9.6 %collective-permute-start.3 = (f32[4,66,1]{2,1,0:T(8,128)S(1)}, f32[4,66,1]{2,1,0:T(8,128)S(1)}, u32[]{:S(2)}, u32[]{:S(2)}) collective-permute-start(f32[4,66,1]{2,1,0:T(8,128)S(1)} %get-tuple-element.211), channel_id=1, source_target_pairs={{2,0},{4,2},{6,4},{8,6},{10,8},{12,10},{14,12},{3,1},{5,3},{7,5},{... | collective-permute-start | bytes 3176 | tf_op jit(solution)/shard_map/while/body/eval_jaxpr/ppermute | solution.py:30
  68.8 10.2 %collective-permute-start.3 = (f32[4,66,1]{2,1,0:T(8,128)S(1)}, f32[4,66,1]{2,1,0:T(8,128)S(1)}, u32[]{:S(2)}, u32[]{:S(2)}) collective-permute-start(f32[4,66,1]{2,1,0:T(8,128)S(1)} %get-tuple-element.211), channel_id=1, source_target_pairs={{2,0},{4,2},{6,4},{8,6},{10,8},{12,10},{14,12},{3,1},{5,3},{7,5},{... | collective-permute-start | bytes 3176 | tf_op jit(solution)/shard_map/while/body/eval_jaxpr/ppermute | solution.py:30
  90.8 8.7 %collective-permute-start.3 = (f32[4,66,1]{2,1,0:T(8,128)S(1)}, f32[4,66,1]{2,1,0:T(8,128)S(1)}, u32[]{:S(2)}, u32[]{:S(2)}) collective-permute-start(f32[4,66,1]{2,1,0:T(8,128)S(1)} %get-tuple-element.211), channel_id=1, source_target_pairs={{2,0},{4,2},{6,4},{8,6},{10,8},{12,10},{14,12},{3,1},{5,3},{7,5},{... | collective-permute-start | bytes 3176 | tf_op jit(solution)/shard_map/while/body/eval_jaxpr/ppermute | solution.py:30
  111.1 8.6 %collective-permute-start.3 = (f32[4,66,1]{2,1,0:T(8,128)S(1)}, f32[4,66,1]{2,1,0:T(8,128)S(1)}, u32[]{:S(2)}, u32[]{:S(2)}) collective-permute-start(f32[4,66,1]{2,1,0:T(8,128)S(1)} %get-tuple-element.211), channel_id=1, source_target_pairs={{2,0},{4,2},{6,4},{8,6},{10,8},{12,10},{14,12},{3,1},{5,3},{7,5},{... | collective-permute-start | bytes 3176 | tf_op jit(solution)/shard_map/while/body/eval_jaxpr/ppermute | solution.py:30
  151.8 8.6 %collective-permute-start.3 = (f32[4,66,1]{2,1,0:T(8,128)S(1)}, f32[4,66,1]{2,1,0:T(8,128)S(1)}, u32[]{:S(2)}, u32[]{:S(2)}) collective-permute-start(f32[4,66,1]{2,1,0:T(8,128)S(1)} %get-tuple-element.211), channel_id=1, source_target_pairs={{2,0},{4,2},{6,4},{8,6},{10,8},{12,10},{14,12},{3,1},{5,3},{7,5},{... | collective-permute-start | bytes 3176 | tf_op jit(solution)/shard_map/while/body/eval_jaxpr/ppermute | solution.py:30
  172.2 8.6 %collective-permute-start.3 = (f32[4,66,1]{2,1,0:T(8,128)S(1)}, f32[4,66,1]{2,1,0:T(8,128)S(1)}, u32[]{:S(2)}, u32[]{:S(2)}) collective-permute-start(f32[4,66,1]{2,1,0:T(8,128)S(1)} %get-tuple-element.211), channel_id=1, source_target_pairs={{2,0},{4,2},{6,4},{8,6},{10,8},{12,10},{14,12},{3,1},{5,3},{7,5},{... | collective-permute-start | bytes 3176 | tf_op jit(solution)/shard_map/while/body/eval_jaxpr/ppermute | solution.py:30
  192.6 8.6 %collective-permute-start.3 = (f32[4,66,1]{2,1,0:T(8,128)S(1)}, f32[4,66,1]{2,1,0:T(8,128)S(1)}, u32[]{:S(2)}, u32[]{:S(2)}) collective-permute-start(f32[4,66,1]{2,1,0:T(8,128)S(1)} %get-tuple-element.211), channel_id=1, source_target_pairs={{2,0},{4,2},{6,4},{8,6},{10,8},{12,10},{14,12},{3,1},{5,3},{7,5},{... | collective-permute-start | bytes 3176 | tf_op jit(solution)/shard_map/while/body/eval_jaxpr/ppermute | solution.py:30
  212.9 8.6 %collective-permute-start.3 = (f32[4,66,1]{2,1,0:T(8,128)S(1)}, f32[4,66,1]{2,1,0:T(8,128)S(1)}, u32[]{:S(2)}, u32[]{:S(2)}) collective-permute-start(f32[4,66,1]{2,1,0:T(8,128)S(1)} %get-tuple-element.211), channel_id=1, source_target_pairs={{2,0},{4,2},{6,4},{8,6},{10,8},{12,10},{14,12},{3,1},{5,3},{7,5},{... | collective-permute-start | bytes 3176 | tf_op jit(solution)/shard_map/while/body/eval_jaxpr/ppermute | solution.py:30
  233.3 8.6 %collective-permute-start.3 = (f32[4,66,1]{2,1,0:T(8,128)S(1)}, f32[4,66,1]{2,1,0:T(8,128)S(1)}, u32[]{:S(2)}, u32[]{:S(2)}) collective-permute-start(f32[4,66,1]{2,1,0:T(8,128)S(1)} %get-tuple-element.211), channel_id=1, source_target_pairs={{2,0},{4,2},{6,4},{8,6},{10,8},{12,10},{14,12},{3,1},{5,3},{7,5},{... | collective-permute-start | bytes 3176 | tf_op jit(solution)/shard_map/while/body/eval_jaxpr/ppermute | solution.py:30
  253.7 8.6 %collective-permute-start.3 = (f32[4,66,1]{2,1,0:T(8,128)S(1)}, f32[4,66,1]{2,1,0:T(8,128)S(1)}, u32[]{:S(2)}, u32[]{:S(2)}) collective-permute-start(f32[4,66,1]{2,1,0:T(8,128)S(1)} %get-tuple-element.211), channel_id=1, source_target_pairs={{2,0},{4,2},{6,4},{8,6},{10,8},{12,10},{14,12},{3,1},{5,3},{7,5},{... | collective-permute-start | bytes 3176 | tf_op jit(solution)/shard_map/while/body/eval_jaxpr/ppermute | solution.py:30
  274.0 8.6 %collective-permute-start.3 = (f32[4,66,1]{2,1,0:T(8,128)S(1)}, f32[4,66,1]{2,1,0:T(8,128)S(1)}, u32[]{:S(2)}, u32[]{:S(2)}) collective-permute-start(f32[4,66,1]{2,1,0:T(8,128)S(1)} %get-tuple-element.211), channel_id=1, source_target_pairs={{2,0},{4,2},{6,4},{8,6},{10,8},{12,10},{14,12},{3,1},{5,3},{7,5},{... | collective-permute-start | bytes 3176 | tf_op jit(solution)/shard_map/while/body/eval_jaxpr/ppermute | solution.py:30
  294.4 8.6 %collective-permute-start.3 = (f32[4,66,1]{2,1,0:T(8,128)S(1)}, f32[4,66,1]{2,1,0:T(8,128)S(1)}, u32[]{:S(2)}, u32[]{:S(2)}) collective-permute-start(f32[4,66,1]{2,1,0:T(8,128)S(1)} %get-tuple-element.211), channel_id=1, source_target_pairs={{2,0},{4,2},{6,4},{8,6},{10,8},{12,10},{14,12},{3,1},{5,3},{7,5},{... | collective-permute-start | bytes 3176 | tf_op jit(solution)/shard_map/while/body/eval_jaxpr/ppermute | solution.py:30
  364.4 15.9 %collective-permute-start.14 = (f32[4,1,256]{2,1,0:T(1,128)S(1)}, f32[4,1,256]{2,1,0:T(1,128)S(1)}, u32[]{:S(2)}, u32[]{:S(2)}) collective-permute-start(f32[4,1,256]{2,1,0:T(1,128)S(1)} %slice.263), channel_id=1, source_target_pairs={{16,0},{32,16},{48,32},{64,48},{80,64},{96,80},{112,96},{128,112},... | collective-permute-start | bytes 12296 | tf_op jit(solution)/shard_map/ppermute | solution.py:17
  366.3 10.6 %collective-permute-start.15 = (f32[4,64,1]{2,1,0:T(8,128)S(1)}, f32[4,64,1]{2,1,0:T(8,128)S(1)}, u32[]{:S(2)}, u32[]{:S(2)}) collective-permute-start(f32[4,64,1]{2,1,0:T(8,128)S(1)} %slice.265), channel_id=1, source_target_pairs={{2,0},{4,2},{6,4},{8,6},{10,8},{12,10},{14,12},{3,1},{5,3},{7,5},{... | collective-permute-start | bytes 3080 | tf_op jit(solution)/shard_map/ppermute | solution.py:17
  376.9 30.7 %collective-permute-start.8 = (f32[32,1,128]{2,0,1:T(8,128)}, f32[32,1,128]{2,0,1:T(8,128)}, u32[]{:S(2)}, u32[]{:S(2)}) collective-permute-start(f32[32,1,128]{2,0,1:T(8,128)} %bitcast.17), channel_id=1, source_target_pairs={{0,16},{16,32},{32,48},{48,64},{64,80},{80,96},{96,112},{112,128},... | collective-permute-start | bytes 49160 | tf_op jit(solution)/shard_map/ppermute | solution.py:28
  385.5 42.9 %all-to-all-start = ((f32[2,1,32768]{2,1,0:T(1,128)}), f32[2,1,32768]{2,1,0:T(1,128)S(1)}, u32[]{:S(2)}, u32[]{:S(2)}) async-start(f32[2,1,32768]{2,1,0:T(1,128)} %reshape.84), calls=%async_computation | async-start | bytes 524288 | tf_op jit(solution)/shard_map/all_to_all | solution.py:130
  400.3 31.2 %collective-permute-start.11 = (f32[32,66,1]{1,0,2:T(8,128)}, f32[32,66,1]{1,0,2:T(8,128)S(1)}, u32[]{:S(2)}, u32[]{:S(2)}) collective-permute-start(f32[32,66,1]{1,0,2:T(8,128)} %get-tuple-element.130), channel_id=1, source_target_pairs={{1,0},{2,1},{3,2},{4,3},{5,4},{6,5},{7,6},{8,7},{9,8},{10,9},{11,1... | collective-permute-start | bytes 25352 | tf_op jit(solution)/shard_map/ppermute | solution.py:30
  402.3 29.3 %collective-permute-start.13 = (f32[32,66,1]{1,0,2:T(8,128)S(1)}, f32[32,66,1]{1,0,2:T(8,128)S(1)}, u32[]{:S(2)}, u32[]{:S(2)}) collective-permute-start(f32[32,66,1]{1,0,2:T(8,128)S(1)} %get-tuple-element.131), channel_id=1, source_target_pairs={{0,1},{1,2},{2,3},{3,4},{4,5},{5,6},{6,7},{7,8},{8,9},{9,10},{10,1... | collective-permute-start | bytes 25352 | tf_op jit(solution)/shard_map/ppermute | solution.py:28
  416.5 15.1 %collective-permute-start.12 = (f32[32,66,1]{1,0,2:T(8,128)}, f32[32,66,1]{1,0,2:T(8,128)}, u32[]{:S(2)}, u32[]{:S(2)}) collective-permute-start(f32[32,66,1]{1,0,2:T(8,128)} %get-tuple-element.128), channel_id=1, source_target_pairs={{0,1},{1,2},{2,3},{3,4},{4,5},{5,6},{6,7},{7,8},{8,9},{9,10},{10,1... | collective-permute-start | bytes 25352 | tf_op jit(solution)/shard_map/ppermute | solution.py:28
  420.4 11.2 %collective-permute-start.10 = (f32[32,66,1]{1,0,2:T(8,128)}, f32[32,66,1]{1,0,2:T(8,128)}, u32[]{:S(2)}, u32[]{:S(2)}) collective-permute-start(f32[32,66,1]{1,0,2:T(8,128)} %get-tuple-element.129), channel_id=1, source_target_pairs={{1,0},{2,1},{3,2},{4,3},{5,4},{6,5},{7,6},{8,7},{9,8},{10,9},{11,1... | collective-permute-start | bytes 25352 | tf_op jit(solution)/shard_map/ppermute | solution.py:30
  463.3 10.2 %collective-permute-start.17 = (f32[32,1,128]{2,0,1:T(8,128)S(1)}, f32[32,1,128]{2,0,1:T(8,128)S(1)}, u32[]{:S(2)}, u32[]{:S(2)}) collective-permute-start(f32[32,1,128]{2,0,1:T(8,128)S(1)} %copy.196), channel_id=1, source_target_pairs={{0,16},{16,32},{32,48},{48,64},{64,80},{80,96},{96,112},{112,128},... | collective-permute-start | bytes 49160 | tf_op jit(solution)/shard_map/ppermute | solution.py:28
  480.1 10.2 %collective-permute-start.18 = (f32[32,66,1]{1,0,2:T(8,128)S(1)}, f32[32,66,1]{1,0,2:T(8,128)S(1)}, u32[]{:S(2)}, u32[]{:S(2)}) collective-permute-start(f32[32,66,1]{1,0,2:T(8,128)S(1)} %get-tuple-element.126), channel_id=1, source_target_pairs={{1,0},{2,1},{3,2},{4,3},{5,4},{6,5},{7,6},{8,7},{9,8},{10,9},{11,1... | collective-permute-start | bytes 25352 | tf_op jit(solution)/shard_map/ppermute | solution.py:30
  507.6 9.0 %collective-permute-start.21 = (f32[32,1,128]{2,0,1:T(8,128)S(1)}, f32[32,1,128]{2,0,1:T(8,128)S(1)}, u32[]{:S(2)}, u32[]{:S(2)}) collective-permute-start(f32[32,1,128]{2,0,1:T(8,128)S(1)} %copy.203), channel_id=1, source_target_pairs={{0,16},{16,32},{32,48},{48,64},{64,80},{80,96},{96,112},{112,128},... | collective-permute-start | bytes 49160 | tf_op jit(solution)/shard_map/ppermute | solution.py:28
  510.8 8.7 %collective-permute-start.20 = (f32[32,1,128]{2,0,1:T(8,128)S(1)}, f32[32,1,128]{2,0,1:T(8,128)S(1)}, u32[]{:S(2)}, u32[]{:S(2)}) collective-permute-start(f32[32,1,128]{2,0,1:T(8,128)S(1)} %copy.201), channel_id=1, source_target_pairs={{16,0},{32,16},{48,32},{64,48},{80,64},{96,80},{112,96},{128,112},... | collective-permute-start | bytes 49160 | tf_op jit(solution)/shard_map/ppermute | solution.py:30
  523.3 9.7 %collective-permute-start.22 = (f32[32,66,1]{1,0,2:T(8,128)S(1)}, f32[32,66,1]{1,0,2:T(8,128)S(1)}, u32[]{:S(2)}, u32[]{:S(2)}) collective-permute-start(f32[32,66,1]{1,0,2:T(8,128)S(1)} %get-tuple-element.124), channel_id=1, source_target_pairs={{1,0},{2,1},{3,2},{4,3},{5,4},{6,5},{7,6},{8,7},{9,8},{10,9},{11,1... | collective-permute-start | bytes 25352 | tf_op jit(solution)/shard_map/ppermute | solution.py:30
  550.8 10.0 %collective-permute-start.25 = (f32[32,1,128]{2,0,1:T(8,128)S(1)}, f32[32,1,128]{2,0,1:T(8,128)S(1)}, u32[]{:S(2)}, u32[]{:S(2)}) collective-permute-start(f32[32,1,128]{2,0,1:T(8,128)S(1)} %copy.210), channel_id=1, source_target_pairs={{0,16},{16,32},{32,48},{48,64},{64,80},{80,96},{96,112},{112,128},... | collective-permute-start | bytes 49160 | tf_op jit(solution)/shard_map/ppermute | solution.py:28
  567.4 9.9 %collective-permute-start.26 = (f32[32,66,1]{1,0,2:T(8,128)S(1)}, f32[32,66,1]{1,0,2:T(8,128)S(1)}, u32[]{:S(2)}, u32[]{:S(2)}) collective-permute-start(f32[32,66,1]{1,0,2:T(8,128)S(1)} %get-tuple-element.122), channel_id=1, source_target_pairs={{1,0},{2,1},{3,2},{4,3},{5,4},{6,5},{7,6},{8,7},{9,8},{10,9},{11,1... | collective-permute-start | bytes 25352 | tf_op jit(solution)/shard_map/ppermute | solution.py:30
  (83 other events, 1060.1 us)
where the time goes:
time: 606 us; the launch traced here: 595 us
  starting transfers between devices  254 us (42%)
  waiting for transfers between devices  159 us (26%)
  other arithmetic  92.2 us (15%)
  local copies, waits for them, and re-layouts  86 us (14%)
    ppermute x42, starting transfers between devices, with_halo(): lax.ppermute(tail, axis, [(i, (i + 1) % count) for i in range(ends)])  135 us
    ppermute x42, waiting for transfers between devices, with_halo(): lax.ppermute(head, axis, [((i + 1) % count, i) for i in range(ends)])  106 us
    ppermute x42, starting transfers between devices, with_halo(): lax.ppermute(head, axis, [((i + 1) % count, i) for i in range(ends)])  100 us
    add x4, other arithmetic, heat_step(): return theta + inv_capacity * (flow + heat)  63.9 us
    ppermute x42, waiting for transfers between devices, with_halo(): lax.ppermute(tail, axis, [(i, (i + 1) % count) for i in range(ends)])  53.1 us
    slice x24, local copies, waits for them, and re-layouts, with_halo(): lax.slice_in_dim(cells, cells.shape[dim] - width, cells.shape[dim], axis=...  18.9 us
    unnamed x56, local copies, waits for them, and re-layouts  16.9 us
    ppermute x5, local copies, waits for them, and re-layouts, with_halo(): lax.ppermute(tail, axis, [(i, (i + 1) % count) for i in range(ends)])  15.8 us
  transfers between devices with their start and end apart: 89, of which 47 were waited for; matrix products, arithmetic and copies ran while one was open for 14% of the time, Pallas kernels for 0%

commit v1 on v0

v1 whole, which is shorter than its diff:
```python
import functools

import jax
import jax.numpy as jnp
from jax import lax
from jax.experimental import pallas as pl
from jax.experimental.pallas import tpu as pltpu
from jax.sharding import PartitionSpec as P

MESH = pl.DeviceIdType.MESH
F32 = jnp.float32
SWEEPS = 16
STEPS = 4
MATERIALS = 4
HALO = 20
PITCH = 24
TOP = 24
V = 13
W = 9
SRC, PAD, GXP, GYP, LEAK = range(5)
DIRS = ((-1, 0), (1, 0), (0, -1), (0, 1), (-1, -1), (-1, 1), (1, -1), (1, 1))


def iota(shape, dim):
    return lax.broadcasted_iota(jnp.int32, shape, dim)


def roll(x, shift, axis):
    return pltpu.roll(x, shift % x.shape[axis], axis)


def inverse(x):
    r = pl.reciprocal(x, approx=True)
    r = r * (2.0 - x * r)
    return r * (2.0 - x * r)


def harmonic(a, b):
    return 2.0 * a * b * inverse(a + b)


def mesh_kernel(
    sizes,
    tidx, tcur, dens, pad, row, col, mat, rates, theta, kappa, invc,
    drop_out, heat_out, trow, tx, ty,
    ext, row_send, row_recv, col_send, xr, yr, coef, raw, usave, nat, unat, trow_send, tcol_send, heat_send,
    ssem, rsem, tssem, trsem, pssem, prsem,
):
    nx, ny, nz = sizes
    gx, gy, gz = lax.axis_index("gx"), lax.axis_index("gy"), lax.axis_index("gz")
    tiers, rows, cols = dens.shape
    nc = ny * nz
    c = gy * nz + gz

    def mesh_to(d):
        dx, dy = DIRS[d]
        return (lax.rem(gx + dx + nx, nx), lax.rem(gy + dy + ny, ny), gz)

    def heat_to(d):
        dx, dy = DIRS[d]
        there = lax.rem(c + dy + nc, nc)
        return (lax.rem(gx + dx + nx, nx), there // nz, lax.rem(there, nz))

    partner = (gx, gy, 1 - gz)

    barrier = pltpu.get_barrier_semaphore()
    for d in range(8):
        pl.semaphore_signal(barrier, inc=1, device_id=mesh_to(d), device_id_type=MESH)
    for d in range(2, 8):
        pl.semaphore_signal(barrier, inc=1, device_id=heat_to(d), device_id_type=MESH)

    def mesh_copy(d, t):
        top, bottom = pl.ds(0, TOP), pl.ds(rows - TOP, TOP)
        if d < 2:
            src, dst = row_send.at[d, t], row_recv.at[d, t]
        elif d == 2:
            src, dst = col_send.at[0, t], xr.at[t, pl.ds(TOP, rows)]
        elif d == 3:
            src, dst = col_send.at[1, t], yr.at[t, pl.ds(TOP, rows)]
        elif d == 4:
            src, dst = col_send.at[0, t, top], xr.at[t, pl.ds(TOP + rows, TOP)]
        elif d == 5:
            src, dst = col_send.at[1, t, top], yr.at[t, pl.ds(TOP + rows, TOP)]
        elif d == 6:
            src, dst = col_send.at[0, t, bottom], xr.at[t, pl.ds(0, TOP)]
        else:
            src, dst = col_send.at[1, t, bottom], yr.at[t, pl.ds(0, TOP)]
        return pltpu.make_async_remote_copy(
            src_ref=src, dst_ref=dst, send_sem=ssem.at[d, t], recv_sem=rsem.at[d, t],
            device_id=mesh_to(d), device_id_type=MESH,
        )

    def heat_copy(d):
        top, bottom = pl.ds(0, 8), pl.ds(rows - 8, 8)
        if d < 2:
            src, dst = trow_send.at[d], trow.at[d]
        elif d == 2:
            src, dst = tcol_send.at[0], tx.at[:, pl.ds(8, rows)]
        elif d == 3:
            src, dst = tcol_send.at[1], ty.at[:, pl.ds(8, rows)]
        elif d == 4:
            src, dst = tcol_send.at[0, :, top], tx.at[:, pl.ds(8 + rows, 8)]
        elif d == 5:
            src, dst = tcol_send.at[1, :, top], ty.at[:, pl.ds(8 + rows, 8)]
        elif d == 6:
            src, dst = tcol_send.at[0, :, bottom], tx.at[:, pl.ds(0, 8)]
        else:
            src, dst = tcol_send.at[1, :, bottom], ty.at[:, pl.ds(0, 8)]
        return pltpu.make_async_remote_copy(
            src_ref=src, dst_ref=dst, send_sem=tssem.at[d], recv_sem=trsem.at[d],
            device_id=heat_to(d), device_id_type=MESH,
        )

    def power_copy(t):
        return pltpu.make_async_remote_copy(
            src_ref=heat_send.at[t], dst_ref=heat_out.at[gz * tiers + t], send_sem=pssem.at[t], recv_sem=prsem.at[t],
            device_id=partner, device_id_type=MESH,
        )

    def prepare(t):
        idx, cur = tidx[t], tcur[t]
        tiles = []
        for b in range(2):
            spot = idx[b : b + 1]
            at_row = jnp.where(iota((rows, 128), 0) == (spot >> 7), cur[b : b + 1], 0.0)
            at_col = jnp.where(iota((128, 128), 0) == (spot & 127), 1.0, 0.0)
            tiles.append(lax.dot_general(
                at_row, at_col, (((1,), (1,)), ((), ())),
                precision=lax.Precision.HIGHEST, preferred_element_type=F32,
            ))
        source = dens[t] + jnp.concatenate(tiles, 1)
        last_row = (iota((rows, cols), 0) == rows - 1) & (gx == nx - 1)
        last_col = (iota((rows, cols), 1) == cols - 1) & (gy == ny - 1)
        gxp = jnp.where(last_row, 0.0, row[t])
        gyp = jnp.where(last_col, 0.0, col[t])
        kinds = mat[t]
        leak = jnp.zeros((rows, cols), F32)
        for kind in range(MATERIALS):
            leak = jnp.where(kinds == kind, rates[kind], leak)
        fields = (source, pad[t], gxp, gyp, leak)
        lane = iota((rows, 128), 1)
        left = right = jnp.zeros((rows, 128), F32)
        for a, field in enumerate(fields):
            for tile in range(2):
                ext[a, t, tile, pl.ds(TOP, rows), :] = field[:, tile * 128 : tile * 128 + 128]
            size = HALO if a < LEAK else 4
            at = a * HALO if a < LEAK else LEAK * HALO
            row_send[0, t, at : at + size, :] = field[:size]
            row_send[1, t, at : at + size, :] = field[rows - size :]
            mine = (lane >= a * PITCH) & (lane < a * PITCH + size)
            left = jnp.where(mine, roll(field[:, :128], a * PITCH, 1), left)
            right = jnp.where(mine, roll(field[:, cols - 128 :], a * PITCH + size, 1), right)
        row_send[0, t, 84:88, :] = jnp.zeros((4, cols), F32)
        row_send[1, t, 84:88, :] = jnp.zeros((4, cols), F32)
        col_send[0, t] = left
        col_send[1, t] = right

    def pack_heat():
        sub = iota((16, 8, 128), 1)
        lane = iota((rows, 128), 1)
        for a, field in enumerate((theta, kappa, invc)):
            one, two = field[0:16, 0:8, :], field[16:32, 0:8, :]
            trow_send[0, a] = jnp.where(sub < 4, one, roll(two, 4, 1))
            one, two = field[0:16, rows - 8 : rows, :], field[16:32, rows - 8 : rows, :]
            trow_send[1, a] = jnp.where(sub < 4, roll(one, 4, 1), two)

            def gather(l, held):
                low, high = held
                mine = (lane >> 3) == l
                shift = lax.rem(8 * l + 4, 128)
                low = jnp.where(mine, pltpu.roll(field[l], shift, 1), low)
                high = jnp.where(mine, pltpu.roll(field[l + 16], shift, 1), high)
                return low, high

            zero = jnp.zeros((rows, 128), F32)
            low, high = lax.fori_loop(0, 16, gather, (zero, zero))
            first = (lane & 7) < 4
            tcol_send[0, a] = jnp.where(first, roll(high, -4, 1), low)
            tcol_send[1, a] = jnp.where(first, low, roll(high, 4, 1))

    def first_tiers(t, carry):
        prepare(t)

        @pl.when(t == 0)
        def _():
            pl.semaphore_wait(barrier, 14)

        for d in range(8):
            mesh_copy(d, t).start()
        return carry

    lax.fori_loop(0, tiers, first_tiers, 0)
    pack_heat()
    for d in range(8):
        heat_copy(d).start()

    lane_ext = iota((8, 384), 1)
    inside = (lane_ext < cols + HALO) | (lane_ext >= 384 - HALO)
    lane = iota((rows + 2 * TOP, 128), 1)
    half = iota((8, 128), 1) < 64

    def tier(t, carry):
        for d in range(8):
            mesh_copy(d, t).wait_recv()
        for a in range(5):
            size = HALO if a < LEAK else 4
            at = a * HALO if a < LEAK else LEAK * HALO
            for tile in range(2):
                part = pl.ds(tile * 128, 128)
                ext[a, t, tile, 0:TOP, :] = jnp.zeros((TOP, 128), F32)
                ext[a, t, tile, TOP - size : TOP, :] = row_recv[1, t, at : at + size, part]
                ext[a, t, tile, TOP + rows :, :] = jnp.zeros((TOP, 128), F32)
                ext[a, t, tile, TOP + rows : TOP + rows + size, :] = row_recv[0, t, at : at + size, part]
            ext[a, t, 2] = jnp.where(
                lane < 64, roll(xr[t], -a * PITCH, 1), roll(yr[t], 128 - size - a * PITCH, 1)
            )

        def load(a, start):
            return jnp.concatenate([ext[a, t, tile, pl.ds(start, 8, stride=V), :] for tile in range(3)], 1)

        def coefficients(v, held):
            start = TOP - HALO + v
            fields = [load(a, start) for a in range(5)]
            src, pd, gxp, gyp, leak = fields
            gxm = load(GXP, start - 1)
            gym = roll(gyp, 1, 1)
            r = jnp.where(inside, inverse(pd + gxp + gxm + gyp + gym), 0.0)
            for i, x in enumerate((src, gxp, gxm, gyp, gym)):
                coef[i, v] = x * r
            for i, x in enumerate((pd, gxp, gyp, leak)):
                raw[i, v] = x
            return held

        lax.fori_loop(0, V, coefficients, 0)

        def next_row(u):
            return jnp.concatenate([u[1:], roll(u[:1], -1, 1)], 0)

        def sweep(count, u):
            below = next_row(u)
            above = jnp.concatenate([roll(u[-1:], 1, 1), u[:-1]], 0)
            flow = coef[1] * below + coef[2] * above
            flow = flow + coef[3] * roll(u, -1, 2) + coef[4] * roll(u, 1, 2)
            return coef[0] + flow

        u = lax.fori_loop(0, SWEEPS - 1, sweep, coef[0])
        across, along = next_row(u) - u, roll(u, -1, 2) - u
        power = raw[0] * u * u + raw[1] * across * across + raw[2] * along * along + raw[3] * jnp.exp(-u)
        usave[0] = u
        usave[1] = power

        def spread(v, held):
            at = pl.ds(TOP - HALO + v, 8, stride=V)
            for tile in range(3):
                if tile < 2:
                    unat[tile, at, :] = usave[0, v, :, tile * 128 : tile * 128 + 128]
                nat[tile, at, :] = usave[1, v, :, tile * 128 : tile * 128 + 128]
            return held

        lax.fori_loop(0, V, spread, 0)
        for tile in range(2):
            drop_out[t, :, tile * 128 : tile * 128 + 128] = unat[tile, TOP : TOP + rows, :]

        def hand(v, held):
            at = pl.ds(TOP - 4 + v, 8, stride=W)

            def pair(z):
                return nat[z, at, :], jnp.where(half, nat[1 + z, at, :], nat[2 - 2 * z, at, :])

            heat_send[t, 0, v], heat_send[t, 1, v] = pair(1 - gz)
            heat_out[gz * tiers + t, 0, v], heat_out[gz * tiers + t, 1, v] = pair(gz)
            return held

        lax.fori_loop(0, W, hand, 0)
        power_copy(t).start()
        return carry

    lax.fori_loop(0, tiers, tier, 0)

    def finish(t, carry):
        for d in range(8):
            mesh_copy(d, t).wait_send()
        pltpu.make_async_remote_copy(
            src_ref=heat_send.at[t], dst_ref=heat_out.at[(1 - gz) * tiers + t], send_sem=pssem.at[t],
            recv_sem=prsem.at[t], device_id=partner, device_id_type=MESH,
        ).wait()
        return carry

    lax.fori_loop(0, tiers, finish, 0)
    for d in range(8):
        heat_copy(d).wait()


def heat_kernel(sizes, theta, kappa, invc, heat, trow, tx, ty, out, nat, temp, cap, lx, ly, lz, onat):
    nx, ny, nz = sizes
    layers, rows, lanes = theta.shape
    gx = lax.axis_index("gx")
    c = lax.axis_index("gy") * nz + lax.axis_index("gz")
    lane = iota((rows + 16, 128), 1)
    first = (lane & 7) < 4

    for a, field in enumerate((theta, kappa, invc)):
        x, y = tx[a], ty[a]
        packs = (jnp.where(first, y, x), jnp.where(first, roll(y, -4, 1), roll(x, 4, 1)))
        for part, pack in enumerate(packs):

            def unpack(l, held, a=a, field=field, part=part, pack=pack):
                layer = part * 16 + l
                above, below = trow[1, a, l], trow[0, a, l]
                nat[a, layer, 0, 0:8, :] = above if part else roll(above, 4, 0)
                nat[a, layer, 0, pl.ds(8, rows), :] = field[layer]
                nat[a, layer, 0, pl.ds(8 + rows, 8), :] = roll(below, 4, 0) if part else below
                nat[a, layer, 1] = pltpu.roll(pack, lax.rem(252 - 8 * l, 128), 1)
                return held

            lax.fori_loop(0, 16, unpack, 0)

    shape = (W, 8, 2 * lanes)
    row_of = iota(shape, 1) * W + iota(shape, 0) - 4
    col_of = iota(shape, 2)
    no_row = ((row_of == rows - 1) & (gx == nx - 1)) | ((row_of == -1) & (gx == 0))
    no_col = ((col_of == lanes - 1) & (c == ny * nz - 1)) | ((col_of == 2 * lanes - 1) & (c == 0))

    def strided(a, layer):
        return jnp.stack([
            jnp.concatenate([nat[a, layer, tile, pl.ds(4 + v, 8, stride=W), :] for tile in range(2)], 1)
            for v in range(W)
        ])

    def next_row(x):
        return jnp.concatenate([x[1:], roll(x[:1], -1, 1)], 0)

    def last_row(x):
        return jnp.concatenate([roll(x[-1:], 1, 1), x[:-1]], 0)

    def links(layer, k):
        temp[layer] = strided(0, layer)
        cap[layer] = strided(2, layer)
        lx[layer] = jnp.where(no_row, 0.0, harmonic(k, next_row(k)))
        ly[layer] = jnp.where(no_col, 0.0, harmonic(k, roll(k, -1, 2)))
        over = strided(1, jnp.minimum(layer + 1, layers - 1))
        lz[layer + 1] = jnp.where(layer == layers - 1, 0.0, harmonic(k, over))
        return over

    ground = strided(1, 0)
    lz[0] = ground
    lax.fori_loop(0, layers, links, ground)

    def step(count, carry):
        def per_tier(tier, below):
            for part in range(4):
                layer = tier * 4 + part
                here = temp[layer]
                fx = lx[layer] * (next_row(here) - here)
                fy = ly[layer] * (roll(here, -1, 2) - here)
                fz = lz[layer + 1] * (temp[jnp.minimum(layer + 1, layers - 1)] - here)
                flow = (fx - last_row(fx)) + (fy - roll(fy, 1, 2)) + (fz - below)
                if part == 0:
                    flow = flow + jnp.concatenate([heat[tier, 0], heat[tier, 1]], 2)
                temp[layer] = here + cap[layer] * flow
                below = fz
            return below

        lax.fori_loop(0, layers // 4, per_tier, lz[0] * temp[0])
        return carry

    lax.fori_loop(0, STEPS, step, 0)

    def result(layer, carry):
        for v in range(W):
            onat[pl.ds(4 + v, 8, stride=W), :] = temp[layer, v, :, 0:lanes]
        out[layer] = onat[pl.ds(8, rows), :]
        return carry

    lax.fori_loop(0, layers, result, 0)


def shards(sizes, density, tap_index, tap_current, pad_cond, row_cond, col_cond, material, leak_rates, theta, kappa, invc):
    tiers, rows, cols = density.shape
    layers, _, lanes = theta.shape
    vmem = pl.BlockSpec(memory_space=pltpu.VMEM)
    tall = rows + 2 * TOP
    dma = pltpu.SemaphoreType.DMA
    taps = tap_index.shape[-1]
    drop, heat, trow, tx, ty = pl.pallas_call(
        functools.partial(mesh_kernel, sizes),
        out_shape=(
            jax.ShapeDtypeStruct((tiers, rows, cols), F32),
            jax.ShapeDtypeStruct((2 * tiers, 2, W, 8, 128), F32),
            jax.ShapeDtypeStruct((2, 3, 16, 8, 128), F32),
            jax.ShapeDtypeStruct((3, rows + 16, 128), F32),
            jax.ShapeDtypeStruct((3, rows + 16, 128), F32),
        ),
        in_specs=[vmem] * 7 + [pl.BlockSpec(memory_space=pltpu.SMEM)] + [vmem] * 3,
        out_specs=(vmem,) * 5,
        scratch_shapes=[
            pltpu.VMEM((5, tiers, 3, tall, 128), F32),
            pltpu.VMEM((2, tiers, 88, cols), F32),
            pltpu.VMEM((2, tiers, 88, cols), F32),
            pltpu.VMEM((2, tiers, rows, 128), F32),
            pltpu.VMEM((tiers, tall, 128), F32),
            pltpu.VMEM((tiers, tall, 128), F32),
            pltpu.VMEM((5, V, 8, 384), F32),
            pltpu.VMEM((4, V, 8, 384), F32),
            pltpu.VMEM((2, V, 8, 384), F32),
            pltpu.VMEM((3, tall, 128), F32),
            pltpu.VMEM((2, tall, 128), F32),
            pltpu.VMEM((2, 3, 16, 8, 128), F32),
            pltpu.VMEM((2, 3, rows, 128), F32),
            pltpu.VMEM((tiers, 2, W, 8, 128), F32),
            dma((8, tiers)), dma((8, tiers)), dma((8,)), dma((8,)), dma((tiers,)), dma((tiers,)),
        ],
        compiler_params=pltpu.CompilerParams(
            collective_id=0, has_side_effects=True, vmem_limit_bytes=48 * 2**20
        ),
        name="mesh_sweeps",
    )(
        tap_index.reshape(tiers, 2, taps), tap_current.reshape(tiers, 2, taps), density, pad_cond, row_cond, col_cond,
        material, leak_rates, theta, kappa, invc,
    )
    block = (W, 8, 2 * lanes)
    temperature = pl.pallas_call(
        functools.partial(heat_kernel, sizes),
        out_shape=jax.ShapeDtypeStruct(theta.shape, F32),
        in_specs=[vmem] * 7,
        out_specs=vmem,
        scratch_shapes=[
            pltpu.VMEM((3, layers, 2, rows + 16, 128), F32),
            pltpu.VMEM((layers, *block), F32),
            pltpu.VMEM((layers, *block), F32),
            pltpu.VMEM((layers, *block), F32),
            pltpu.VMEM((layers, *block), F32),
            pltpu.VMEM((layers + 1, *block), F32),
            pltpu.VMEM((rows + 16, 128), F32),
        ],
        compiler_params=pltpu.CompilerParams(vmem_limit_bytes=48 * 2**20),
        name="heat_steps",
    )(theta, kappa, invc, heat, trow, tx, ty)
    return drop, temperature


def solution(mesh):
    sizes = tuple(mesh.shape[name] for name in ("gx", "gy", "gz"))
    field = P("gz", "gx", "gy")
    tap = P("gz", "gx", "gy", None)
    block = P(None, "gx", ("gy", "gz"))
    return jax.shard_map(
        functools.partial(shards, sizes),
        mesh=mesh,
        in_specs=(field, tap, tap, field, field, field, field, P(), block, block, block),
        out_specs=(field, block),
        check_vma=False,
    )
```

time: 606 us -> 73 us (0.12)
  the two profiles are of different devices: /device:TPU:103 before, /device:TPU:8 now
where the time goes in v1:
time: 73 us; the launch traced here: 72.3 us
  Pallas kernels  60.4 us (83%)
  local copies, waits for them, and re-layouts  11.2 us (15%)
    pallas_call x1, Pallas kernels, shards(): pl.pallas_call(functools.partial(mesh_kernel, sizes), out_shape=(jax.Shap...  37.3 us
    pallas_call x1, Pallas kernels, shards(): pl.pallas_call(functools.partial(heat_kernel, sizes), out_shape=jax.Shape...  23.1 us
    unnamed x29, local copies, waits for them, and re-layouts  11.2 us

profile of v1, /device:TPU:8, one launch (start us, length us, event | category | flops | bytes accessed | tf_op | source)
XLA Modules:
  0.0 72.3 jit_solution(16671446321798272277)
XLA Ops:
  0.6 0.0 copy-start.13
  0.6 0.6 copy-done.13
  1.3 0.0 copy-start
  1.3 1.2 %copy-done = f32[32,64,128]{2,1,0:T(8,128)S(1)} copy-done((f32[32,64,128]{2,1,0:T(8,128)S(1)}, f32[32,64,128]{2,1,0:T(8,128)}, u32[]{:S(2)}) %copy-start) | copy-done | bytes 1048600
  2.5 0.0 copy-start.2
  2.5 1.2 %copy-done.2 = f32[32,64,128]{2,1,0:T(8,128)S(1)} copy-done((f32[32,64,128]{2,1,0:T(8,128)S(1)}, f32[32,64,128]{2,1,0:T(8,128)}, u32[]{:S(2)}) %copy-start.2) | copy-done | bytes 1048600
  3.7 0.0 copy-start.4
  3.7 1.2 %copy-done.4 = f32[32,64,128]{2,1,0:T(8,128)S(1)} copy-done((f32[32,64,128]{2,1,0:T(8,128)S(1)}, f32[32,64,128]{2,1,0:T(8,128)}, u32[]{:S(2)}) %copy-start.4) | copy-done | bytes 1048600
  5.0 0.0 copy-start.6
  5.0 0.9 %copy-done.6 = f32[4,64,256]{2,1,0:T(8,128)S(1)} copy-done((f32[4,64,256]{2,1,0:T(8,128)S(1)}, f32[4,64,256]{2,1,0:T(8,128)}, u32[]{:S(2)}) %copy-start.6) | copy-done | bytes 262168
  5.9 0.0 copy-start.7
  5.9 0.9 %copy-done.7 = f32[4,64,256]{2,1,0:T(8,128)S(1)} copy-done((f32[4,64,256]{2,1,0:T(8,128)S(1)}, f32[4,64,256]{2,1,0:T(8,128)}, u32[]{:S(2)}) %copy-start.7) | copy-done | bytes 262168
  6.9 0.0 copy-start.8
  6.9 0.9 %copy-done.8 = f32[4,64,256]{2,1,0:T(8,128)S(1)} copy-done((f32[4,64,256]{2,1,0:T(8,128)S(1)}, f32[4,64,256]{2,1,0:T(8,128)}, u32[]{:S(2)}) %copy-start.8) | copy-done | bytes 262168
  7.8 0.0 copy-start.9
  7.8 0.9 %copy-done.9 = f32[4,64,256]{2,1,0:T(8,128)S(1)} copy-done((f32[4,64,256]{2,1,0:T(8,128)S(1)}, f32[4,64,256]{2,1,0:T(8,128)}, u32[]{:S(2)}) %copy-start.9) | copy-done | bytes 262168
  8.8 0.0 copy-start.10
  8.8 0.9 %copy-done.10 = s32[4,64,256]{2,1,0:T(8,128)S(1)} copy-done((s32[4,64,256]{2,1,0:T(8,128)S(1)}, s32[4,64,256]{2,1,0:T(8,128)}, u32[]{:S(2)}) %copy-start.10) | copy-done | bytes 262168
  9.7 0.0 copy-start.11
  9.7 0.7 copy-done.11
  10.4 0.0 copy-start.12
  10.4 0.7 copy-done.12
  11.1 0.0 copy-start.1
  11.1 0.0 copy-start.3
  11.1 0.0 copy-start.5
  11.1 37.3 %mesh_sweeps.1 = (f32[4,64,256]{2,1,0:T(8,128)S(1)}, f32[8,2,9,8,128]{4,3,2,1,0:T(8,128)S(1)}, f32[2,3,16,8,128]{4,3,2,1,0:T(8,128)S(1)}, f32[3,80,128]{2,1,0:T(8,128)S(1)}, f32[3,80,128]{2,1,0:T(8,128)S(1)}) custom-call(s32[4,2,128]{2,1,0:T(2,128)S(1)} %bitcast.2, f32[4,2,128]{2,1,0:T(2,128)S(1)} %bitcast.3, f32[4,64,256]{2,1,0:T(8,128)S(1)} %copy-done.6, ...), custom_call_target="tpu_custom_call" | custom-call | tf_op jit(solution)/shard_map/mesh_sweeps/pallas_call | solution.py:385
  48.4 0.0 copy-done.1
  48.4 0.0 copy-done.3
  48.4 0.0 copy-done.5
  48.4 23.1 %heat_steps.1 = f32[32,64,128]{2,1,0:T(8,128)} custom-call(f32[32,64,128]{2,1,0:T(8,128)S(1)} %copy-done.1, f32[32,64,128]{2,1,0:T(8,128)S(1)} %copy-done.3, f32[32,64,128]{2,1,0:T(8,128)S(1)} %copy-done.5, f32[8,2,9,8,128]{4,3,2,1,0:T(8,128)S(1)} %get-tuple-element.8.heat, f32[2,3,16,8,128]{4,3,2,1,0:T(8,128)S(1)} %get-tuple-element.9.trow, ...), custom_call_target="tpu_custom_call" | custom-call | tf_op jit(solution)/shard_map/heat_steps/pallas_call | solution.py:422
  71.6 0.7 copy.14
Async XLA Ops:
  0.6 0.7 copy-start.13
  1.3 1.2 %copy-start = (f32[32,64,128]{2,1,0:T(8,128)S(1)}, f32[32,64,128]{2,1,0:T(8,128)}, u32[]{:S(2)}) copy-start(f32[32,64,128]{2,1,0:T(8,128)} %theta.3) | copy-start | bytes 3145732
  2.5 1.2 %copy-start.2 = (f32[32,64,128]{2,1,0:T(8,128)S(1)}, f32[32,64,128]{2,1,0:T(8,128)}, u32[]{:S(2)}) copy-start(f32[32,64,128]{2,1,0:T(8,128)} %kappa.3) | copy-start | bytes 3145732
  3.7 1.2 %copy-start.4 = (f32[32,64,128]{2,1,0:T(8,128)S(1)}, f32[32,64,128]{2,1,0:T(8,128)}, u32[]{:S(2)}) copy-start(f32[32,64,128]{2,1,0:T(8,128)} %invc.3) | copy-start | bytes 3145732
  5.0 0.9 %copy-start.6 = (f32[4,64,256]{2,1,0:T(8,128)S(1)}, f32[4,64,256]{2,1,0:T(8,128)}, u32[]{:S(2)}) copy-start(f32[4,64,256]{2,1,0:T(8,128)} %dens.1) | copy-start | bytes 786436
  5.9 0.9 %copy-start.7 = (f32[4,64,256]{2,1,0:T(8,128)S(1)}, f32[4,64,256]{2,1,0:T(8,128)}, u32[]{:S(2)}) copy-start(f32[4,64,256]{2,1,0:T(8,128)} %pad.1) | copy-start | bytes 786436
  6.9 0.9 %copy-start.8 = (f32[4,64,256]{2,1,0:T(8,128)S(1)}, f32[4,64,256]{2,1,0:T(8,128)}, u32[]{:S(2)}) copy-start(f32[4,64,256]{2,1,0:T(8,128)} %row.1) | copy-start | bytes 786436
  7.8 0.9 %copy-start.9 = (f32[4,64,256]{2,1,0:T(8,128)S(1)}, f32[4,64,256]{2,1,0:T(8,128)}, u32[]{:S(2)}) copy-start(f32[4,64,256]{2,1,0:T(8,128)} %col.1) | copy-start | bytes 786436
  8.8 0.9 %copy-start.10 = (s32[4,64,256]{2,1,0:T(8,128)S(1)}, s32[4,64,256]{2,1,0:T(8,128)}, u32[]{:S(2)}) copy-start(s32[4,64,256]{2,1,0:T(8,128)} %mat.1) | copy-start | bytes 786436
  9.7 0.7 copy-start.11
  10.4 0.7 copy-start.12
  11.1 37.3 %copy-start.1 = (f32[32,64,128]{2,1,0:T(8,128)S(1)}, f32[32,64,128]{2,1,0:T(8,128)}, u32[]{:S(2)}) copy-start(f32[32,64,128]{2,1,0:T(8,128)} %theta.3) | copy-start | bytes 3145732
  11.1 37.3 %copy-start.3 = (f32[32,64,128]{2,1,0:T(8,128)S(1)}, f32[32,64,128]{2,1,0:T(8,128)}, u32[]{:S(2)}) copy-start(f32[32,64,128]{2,1,0:T(8,128)} %kappa.3) | copy-start | bytes 3145732
  11.1 37.3 %copy-start.5 = (f32[32,64,128]{2,1,0:T(8,128)S(1)}, f32[32,64,128]{2,1,0:T(8,128)}, u32[]{:S(2)}) copy-start(f32[32,64,128]{2,1,0:T(8,128)} %invc.3) | copy-start | bytes 3145732

commit v2 on v1

v2 whole, which is shorter than its diff:
```python
import functools

import jax
import jax.numpy as jnp
from jax import lax
from jax.experimental import pallas as pl
from jax.experimental.pallas import tpu as pltpu
from jax.sharding import PartitionSpec as P

MESH = pl.DeviceIdType.MESH
F32 = jnp.float32
SWEEPS = 16
STEPS = 4
MATERIALS = 4
HALO = 20
PITCH = 24
TOP = 24
V = 13
W = 9
SRC, PAD, GXP, GYP, LEAK = range(5)
DIRS = ((-1, 0), (1, 0), (0, -1), (0, 1), (-1, -1), (-1, 1), (1, -1), (1, 1))


def iota(shape, dim):
    return lax.broadcasted_iota(jnp.int32, shape, dim)


def roll(x, shift, axis):
    return pltpu.roll(x, shift % x.shape[axis], axis)


def harmonic(a, b):
    total = a + b
    r = pl.reciprocal(total, approx=True)
    r = r * (2.0 - total * r)
    r = r * (2.0 - total * r)
    return 2.0 * a * b * r


def inverse_root(x):
    r = lax.rsqrt(x)
    return r * (1.5 - 0.5 * x * r * r)


def next_row(x):
    return jnp.concatenate([x[1:], roll(x[:1], -1, 1)], 0)


def last_row(x):
    return jnp.concatenate([roll(x[-1:], 1, 1), x[:-1]], 0)


def kernel(
    sizes,
    tidx_hbm, tcur_hbm, dens_hbm, pad_hbm, row_hbm, col_hbm, mat_hbm, rates, theta_hbm, kappa_hbm, invc_hbm,
    drop_out, temp_out,
    tidx, tcur, mat, ext, row_send, row_recv, col_send, xr, yr, coef, raw, ub, nat, unat,
    field, trow_send, trow, tcol_send, tx, ty, edge, heat_send, heat,
    temp, cap, lx, ly, lz, snat, stemp, scap, slx, sly, slz, sground, sheat, mix, onat,
    isem, ssem, rsem, tssem, trsem, pssem, prsem,
):
    nx, ny, nz = sizes
    gx, gy, gz = lax.axis_index("gx"), lax.axis_index("gy"), lax.axis_index("gz")
    tiers, rows, cols = drop_out.shape
    layers = temp_out.shape[0]
    nc = ny * nz
    c = gy * nz + gz

    loads = [pltpu.make_async_copy(tidx_hbm, tidx, isem.at[0]), pltpu.make_async_copy(tcur_hbm, tcur, isem.at[1])]
    for a, ref in enumerate((dens_hbm, pad_hbm, row_hbm, col_hbm)):
        for tile in range(2):
            loads.append(pltpu.make_async_copy(
                ref.at[:, :, pl.ds(tile * 128, 128)], ext.at[a, :, tile, pl.ds(TOP, rows)], isem.at[len(loads)]
            ))
    loads.append(pltpu.make_async_copy(mat_hbm, mat, isem.at[len(loads)]))
    heat_loads = [
        pltpu.make_async_copy(ref, field.at[a, :, pl.ds(8, rows)], isem.at[len(loads) + a])
        for a, ref in enumerate((theta_hbm, kappa_hbm, invc_hbm))
    ]
    for load in loads + heat_loads:
        load.start()

    def mesh_to(d):
        dx, dy = DIRS[d]
        return (lax.rem(gx + dx + nx, nx), lax.rem(gy + dy + ny, ny), gz)

    def heat_to(d):
        dx, dy = DIRS[d]
        there = lax.rem(c + dy + nc, nc)
        return (lax.rem(gx + dx + nx, nx), there // nz, lax.rem(there, nz))

    partner = (gx, gy, 1 - gz)

    barrier = pltpu.get_barrier_semaphore()
    for d in range(8):
        pl.semaphore_signal(barrier, inc=1, device_id=mesh_to(d), device_id_type=MESH)
    for d in range(2, 8):
        pl.semaphore_signal(barrier, inc=1, device_id=heat_to(d), device_id_type=MESH)

    def mesh_copy(d, t):
        top, bottom = pl.ds(0, TOP), pl.ds(rows - TOP, TOP)
        if d < 2:
            src, dst = row_send.at[d, t], row_recv.at[d, t]
        elif d == 2:
            src, dst = col_send.at[0, t], xr.at[t, pl.ds(TOP, rows)]
        elif d == 3:
            src, dst = col_send.at[1, t], yr.at[t, pl.ds(TOP, rows)]
        elif d == 4:
            src, dst = col_send.at[0, t, top], xr.at[t, pl.ds(TOP + rows, TOP)]
        elif d == 5:
            src, dst = col_send.at[1, t, top], yr.at[t, pl.ds(TOP + rows, TOP)]
        elif d == 6:
            src, dst = col_send.at[0, t, bottom], xr.at[t, pl.ds(0, TOP)]
        else:
            src, dst = col_send.at[1, t, bottom], yr.at[t, pl.ds(0, TOP)]
        return pltpu.make_async_remote_copy(
            src_ref=src, dst_ref=dst, send_sem=ssem.at[d, t], recv_sem=rsem.at[d, t],
            device_id=mesh_to(d), device_id_type=MESH,
        )

    def heat_copy(d):
        top, bottom = pl.ds(0, 8), pl.ds(rows - 8, 8)
        if d < 2:
            src, dst = trow_send.at[d], trow.at[d]
        elif d == 2:
            src, dst = tcol_send.at[0], tx.at[:, pl.ds(8, rows)]
        elif d == 3:
            src, dst = tcol_send.at[1], ty.at[:, pl.ds(8, rows)]
        elif d == 4:
            src, dst = tcol_send.at[0, :, top], tx.at[:, pl.ds(8 + rows, 8)]
        elif d == 5:
            src, dst = tcol_send.at[1, :, top], ty.at[:, pl.ds(8 + rows, 8)]
        elif d == 6:
            src, dst = tcol_send.at[0, :, bottom], tx.at[:, pl.ds(0, 8)]
        else:
            src, dst = tcol_send.at[1, :, bottom], ty.at[:, pl.ds(0, 8)]
        return pltpu.make_async_remote_copy(
            src_ref=src, dst_ref=dst, send_sem=tssem.at[d], recv_sem=trsem.at[d],
            device_id=heat_to(d), device_id_type=MESH,
        )

    def power_copy(t, z):
        return pltpu.make_async_remote_copy(
            src_ref=heat_send.at[t], dst_ref=heat.at[z * tiers + t], send_sem=pssem.at[t], recv_sem=prsem.at[t],
            device_id=partner, device_id_type=MESH,
        )

    def prepare(t):
        idx, cur = tidx[t], tcur[t]
        main = pl.ds(TOP, rows)
        lane = iota((rows, 128), 1)
        end_row = (iota((rows, 128), 0) == rows - 1) & (gx == nx - 1)
        end_col = (lane == 127) & (gy == ny - 1)
        edges = []
        for tile in range(2):
            spot = idx[tile : tile + 1]
            at_row = jnp.where(iota((rows, 128), 0) == (spot >> 7), cur[tile : tile + 1], 0.0)
            at_col = jnp.where(iota((128, 128), 0) == (spot & 127), 1.0, 0.0)
            taps = lax.dot_general(
                at_row, at_col, (((1,), (1,)), ((), ())),
                precision=lax.Precision.HIGHEST, preferred_element_type=F32,
            )
            source = ext[SRC, t, tile, main, :] + taps
            pad = ext[PAD, t, tile, main, :]
            gxp = jnp.where(end_row, 0.0, ext[GXP, t, tile, main, :])
            gyp = ext[GYP, t, tile, main, :]
            if tile == 1:
                gyp = jnp.where(end_col, 0.0, gyp)
            kinds = mat[t, :, tile * 128 : tile * 128 + 128]
            leak = jnp.zeros((rows, 128), F32)
            for kind in range(MATERIALS):
                leak = jnp.where(kinds == kind, rates[kind], leak)
            ext[SRC, t, tile, main, :] = source
            ext[GXP, t, tile, main, :] = gxp
            ext[GYP, t, tile, main, :] = gyp
            ext[LEAK, t, tile, main, :] = leak
            packed = jnp.zeros((rows, 128), F32)
            part = pl.ds(tile * 128, 128)
            for a, values in enumerate((source, pad, gxp, gyp, leak)):
                size = HALO if a < LEAK else 4
                at = a * HALO if a < LEAK else LEAK * HALO
                row_send[0, t, at : at + size, part] = values[:size]
                row_send[1, t, at : at + size, part] = values[rows - size :]
                mine = (lane >= a * PITCH) & (lane < a * PITCH + size)
                packed = jnp.where(mine, roll(values, a * PITCH + (size if tile else 0), 1), packed)
            row_send[0, t, 84:88, part] = jnp.zeros((4, 128), F32)
            row_send[1, t, 84:88, part] = jnp.zeros((4, 128), F32)
            col_send[tile, t] = packed

    def first_tiers(t, carry):
        prepare(t)

        @pl.when(t == 0)
        def _():
            pl.semaphore_wait(barrier, 14)

        for d in range(8):
            mesh_copy(d, t).start()
        return carry

    for load in loads:
        load.wait()
    lax.fori_loop(0, tiers, first_tiers, 0)

    lane_tall = iota((rows, 128), 1)
    sub = iota((16, 8, 128), 1)
    main = pl.ds(8, rows)
    for load in heat_loads:
        load.wait()
    for a in range(3):
        one, two = field[a, 0:16, 8:16, :], field[a, 16:32, 8:16, :]
        trow_send[0, a] = jnp.where(sub < 4, one, roll(two, 4, 1))
        one, two = field[a, 0:16, rows : rows + 8, :], field[a, 16:32, rows : rows + 8, :]
        trow_send[1, a] = jnp.where(sub < 4, roll(one, 4, 1), two)

    def gather(a, carry):
        low = high = jnp.zeros((rows, 128), F32)
        for l in range(16):
            mine = (lane_tall >> 3) == l
            low = jnp.where(mine, roll(field[a, l, main, :], 8 * l + 4, 1), low)
            high = jnp.where(mine, roll(field[a, l + 16, main, :], 8 * l + 4, 1), high)
        first = (lane_tall & 4) == 0
        tcol_send[0, a] = jnp.where(first, roll(high, -4, 1), low)
        tcol_send[1, a] = jnp.where(first, low, roll(high, 4, 1))
        edge[a, 0, main, :] = low
        edge[a, 1, main, :] = high
        return carry

    lax.fori_loop(0, 3, gather, 0)
    for d in range(8):
        heat_copy(d).start()

    lane_ext = iota((8, 384), 1)
    inside = (lane_ext < cols + HALO) | (lane_ext >= 384 - HALO)
    lane_rows = iota((rows + 2 * TOP, 128), 1)
    half = iota((8, 128), 1) < 64

    def tier(t, carry):
        for d in range(8):
            mesh_copy(d, t).wait_recv()
        for a in range(5):
            size = HALO if a < LEAK else 4
            at = a * HALO if a < LEAK else LEAK * HALO
            for tile in range(2):
                part = pl.ds(tile * 128, 128)
                ext[a, t, tile, 0:8, :] = jnp.zeros((8, 128), F32)
                ext[a, t, tile, TOP - size : TOP, :] = row_recv[1, t, at : at + size, part]
                ext[a, t, tile, TOP + rows : TOP + rows + size, :] = row_recv[0, t, at : at + size, part]
                if a == LEAK:
                    ext[a, t, tile, 8 : TOP - size, :] = jnp.zeros((TOP - size - 8, 128), F32)
                    ext[a, t, tile, TOP + rows + size :, :] = jnp.zeros((TOP - size, 128), F32)
            ext[a, t, 2] = jnp.where(
                lane_rows < 64, roll(xr[t], -a * PITCH, 1), roll(yr[t], 128 - size - a * PITCH, 1)
            )

        def fetch(a, start):
            return jnp.concatenate([ext[a, t, tile, pl.ds(start, 8, stride=V), :] for tile in range(3)], 1)

        roots, gxm = [], fetch(GXP, TOP - HALO - 1)
        for v in range(V):
            src, pd, gxp, gyp, leak = [fetch(a, TOP - HALO + v) for a in range(5)]
            r = jnp.where(inside, inverse_root(pd + gxp + gxm + gyp + roll(gyp, 1, 1)), 0.0)
            gxm = gxp
            for i, x in enumerate((pd, gxp, gyp, leak, r)):
                raw[i, v] = x
            coef[0, v] = src * r
            coef[2, v] = gyp * r * roll(r, -1, 1)
        for v in range(V):
            after = raw[4, v + 1] if v < V - 1 else roll(raw[4, 0], -1, 0)
            coef[1, v] = raw[1, v] * raw[4, v] * after
        coef[1, V] = roll(coef[1, V - 1], 1, 0)

        def sweep(source_of, out):
            here = source_of(0)
            before, link_before = roll(source_of(V - 1), 1, 0), coef[1, V]
            for v in range(V):
                after = source_of(v + 1) if v < V - 1 else roll(source_of(0), -1, 0)
                link, side = coef[1, v], coef[2, v]
                flow = link * after + link_before * before
                flow = flow + (side * roll(here, -1, 1) + roll(side * here, 1, 1))
                ub[out, v] = coef[0, v] + flow
                before, here, link_before = here, after, link

        sweep(lambda v: coef[0, v], 0)

        def two_sweeps(count, held):
            sweep(lambda v: ub[0, v], 1)
            sweep(lambda v: ub[1, v], 0)
            return held

        lax.fori_loop(0, (SWEEPS - 2) // 2, two_sweeps, 0)
        here = first = ub[0, 0] * raw[4, 0]
        for v in range(V):
            after = ub[0, v + 1] * raw[4, v + 1] if v < V - 1 else roll(first, -1, 0)
            across, along = after - here, roll(here, -1, 1) - here
            power = raw[0, v] * here * here + raw[1, v] * across * across + raw[2, v] * along * along
            power = power + raw[3, v] * jnp.exp(-here)
            at = pl.ds(TOP - HALO + v, 8, stride=V)
            for tile in range(3):
                nat[tile, at, :] = power[:, tile * 128 : tile * 128 + 128]
                if tile < 2:
                    unat[tile, at, :] = here[:, tile * 128 : tile * 128 + 128]
            here = after

        for v in range(W):
            at = pl.ds(TOP - 4 + v, 8, stride=W)
            for z, into in ((1 - gz, heat_send.at[t]), (gz, heat.at[gz * tiers + t])):
                into[0, v] = nat[z, at, :]
                into[1, v] = jnp.where(half, nat[1 + z, at, :], nat[2 - 2 * z, at, :])
        power_copy(t, gz).start()
        for tile in range(2):
            drop_out[t, :, tile * 128 : tile * 128 + 128] = unat[tile, TOP : TOP + rows, :]
        return carry

    lax.fori_loop(0, tiers, tier, 0)

    for d in range(8):
        heat_copy(d).wait_recv()
    lane8 = iota((8, 128), 1)
    lane_tall = iota((rows + 16, 128), 1)
    first = (lane_tall & 4) == 0

    def assemble(a, carry):
        above, below = trow[1, a], trow[0, a]
        field[a, 0:16, 0:8, :] = roll(above, 4, 1)
        field[a, 16:32, 0:8, :] = above
        field[a, 0:16, 8 + rows : 16 + rows, :] = below
        field[a, 16:32, 8 + rows : 16 + rows, :] = roll(below, 4, 1)
        up = down = jnp.zeros((8, 128), F32)
        for l in range(16):
            mine = (lane8 >> 3) == l
            up = jnp.where(mine, roll(above[l], 8 * l + 4, 1), up)
            down = jnp.where(mine, roll(below[l], 8 * l + 4, 1), down)
        edge[a, 0, 0:8, :] = roll(up, 4, 0)
        edge[a, 1, 0:8, :] = up
        edge[a, 0, 8 + rows : 16 + rows, :] = down
        edge[a, 1, 8 + rows : 16 + rows, :] = roll(down, 4, 0)
        x, y, low, high = tx[a], ty[a], edge[a, 0], edge[a, 1]
        snat[a, 0] = jnp.where(first, y, low)
        snat[a, 1] = jnp.where(first, low, x)
        snat[a, 2] = jnp.where(first, roll(y, -4, 1), high)
        snat[a, 3] = jnp.where(first, high, roll(x, 4, 1))
        return carry

    lax.fori_loop(0, 3, assemble, 0)

    shape = (W, 8, 128)
    row_of = iota(shape, 1) * W + iota(shape, 0) - 4
    lane = iota(shape, 2)
    no_row = ((row_of == rows - 1) & (gx == nx - 1)) | ((row_of == -1) & (gx == 0))
    no_col = (lane == 127) & (c == nc - 1)

    def strided(ref):
        return jnp.stack([ref[pl.ds(4 + v, 8, stride=W), :] for v in range(W)])

    def upper(low, high):
        return jnp.where(lane < 120, roll(low, -8, 2), roll(high, -8, 2)), roll(high, -8, 2)

    def align(x, layer):
        return pltpu.roll(x, lax.rem(252 - 8 * lax.rem(layer, 16), 128), 2)

    for side in range(2):
        k = [strided(snat.at[1, 2 * h + side]) for h in range(2)]
        over = upper(*k)
        no_edge = ((lane & 7) == 3) & (c == (nc - 1 if side else 0))
        sground[side] = k[0]
        for h in range(2):
            s = 2 * h + side
            stemp[s] = strided(snat.at[0, s])
            scap[s] = strided(snat.at[2, s])
            slx[s] = jnp.where(no_row, 0.0, harmonic(k[h], next_row(k[h])))
            sly[s] = jnp.where(no_edge, 0.0, harmonic(k[h], roll(k[h], -1, 2)))
            link = harmonic(k[h], over[h])
            slz[s] = jnp.where(lane < 120, link, 0.0) if h else link
            if side:
                mix[h] = k[h]

    def links(layer, k):
        temp[layer] = strided(field.at[0, layer])
        cap[layer] = strided(field.at[2, layer])
        over = strided(field.at[1, jnp.minimum(layer + 1, layers - 1)])
        beside = roll(jnp.where(lane == 0, align(mix[layer // 16], layer), k), -1, 2)
        lx[layer] = jnp.where(no_row, 0.0, harmonic(k, next_row(k)))
        ly[layer] = jnp.where(no_col, 0.0, harmonic(k, beside))
        lz[layer + 1] = jnp.where(layer == layers - 1, 0.0, harmonic(k, over))
        return over

    ground = strided(field.at[1, 0])
    lz[0] = ground
    lax.fori_loop(0, layers, links, ground)

    for t in range(tiers):
        power_copy(t, 1 - gz).wait()

    for h in range(2):
        left = right = jnp.zeros(shape, F32)
        for t in range(4):
            inner, outer = heat[h * 4 + t, 0], heat[h * 4 + t, 1]
            mine = (lane >> 3) == 4 * t
            left = jnp.where(mine, roll(jnp.where(lane < 64, inner, outer), 32 * t + 4, 2), left)
            right = jnp.where(mine, roll(jnp.where(lane < 64, outer, inner), 32 * t + 4, 2), right)
        sheat[2 * h] = left
        sheat[2 * h + 1] = right

    def step(count, carry):
        for side in range(2):
            old = [stemp[side], stemp[2 + side]]
            over = upper(*old)
            rise = [slz[2 * h + side] * (over[h] - old[h]) for h in range(2)]
            under = (
                jnp.where(lane < 8, sground[side] * old[0], roll(rise[0], 8, 2)),
                jnp.where(lane < 8, roll(rise[0], 8, 2), roll(rise[1], 8, 2)),
            )
            for h in range(2):
                s = 2 * h + side
                here = old[h]
                fx = slx[s] * (next_row(here) - here)
                fy = sly[s] * (roll(here, -1, 2) - here)
                flow = (fx - last_row(fx)) + (fy - roll(fy, 1, 2)) + (rise[h] - under[h]) + sheat[s]
                stemp[s] = here + scap[s] * flow
                mix[h] = jnp.where((lane & 7) == 3, mix[h], here) if side else fy

        def per_tier(tier, below):
            for part in range(4):
                layer = tier * 4 + part
                here = temp[layer]
                beyond = align(mix[tier // 4], layer)
                fx = lx[layer] * (next_row(here) - here)
                fy = ly[layer] * (roll(jnp.where(lane == 0, beyond, here), -1, 2) - here)
                fz = lz[layer + 1] * (temp[jnp.minimum(layer + 1, layers - 1)] - here)
                before = roll(jnp.where(lane == 127, beyond, fy), 1, 2)
                flow = (fx - last_row(fx)) + (fy - before) + (fz - below)
                if part == 0:
                    flow = flow + heat[tier, 0]
                temp[layer] = here + cap[layer] * flow
                below = fz
            return below

        lax.fori_loop(0, layers // 4, per_tier, lz[0] * temp[0])
        return carry

    lax.fori_loop(0, STEPS, step, 0)

    def result(layer, carry):
        for v in range(W):
            onat[layer, pl.ds(4 + v, 8, stride=W), :] = temp[layer, v]
        temp_out[layer] = onat[layer, pl.ds(8, rows), :]
        return carry

    lax.fori_loop(0, layers, result, 0, unroll=4)

    def finish(t, carry):
        for d in range(8):
            mesh_copy(d, t).wait_send()
        return carry

    lax.fori_loop(0, tiers, finish, 0)
    for d in range(8):
        heat_copy(d).wait_send()


def shards(sizes, density, tap_index, tap_current, pad_cond, row_cond, col_cond, material, leak_rates, theta, kappa, invc):
    tiers, rows, cols = density.shape
    layers = theta.shape[0]
    vmem, hbm = pl.BlockSpec(memory_space=pltpu.VMEM), pl.BlockSpec(memory_space=pl.ANY)
    tall, high = rows + 2 * TOP, rows + 16
    dma = pltpu.SemaphoreType.DMA
    taps = tap_index.shape[-1]
    scratch = [
        (5, tiers, 3, tall, 128),
        (2, tiers, 88, cols), (2, tiers, 88, cols), (2, tiers, rows, 128),
        (tiers, tall, 128), (tiers, tall, 128),
        (3, V + 1, 8, 384), (5, V, 8, 384), (2, V, 8, 384),
        (3, tall, 128), (2, tall, 128),
        (3, layers, high, 128),
        (2, 3, 16, 8, 128), (2, 3, 16, 8, 128),
        (2, 3, rows, 128), (3, high, 128), (3, high, 128), (3, 2, high, 128),
        (tiers, 2, W, 8, 128), (2 * tiers, 2, W, 8, 128),
        (layers, W, 8, 128), (layers, W, 8, 128),
        (layers, W, 8, 128), (layers, W, 8, 128), (layers + 1, W, 8, 128),
        (3, 4, high, 128),
        (4, W, 8, 128), (4, W, 8, 128), (4, W, 8, 128), (4, W, 8, 128), (4, W, 8, 128),
        (2, W, 8, 128), (4, W, 8, 128), (2, W, 8, 128),
        (layers, high, 128),
    ]
    return pl.pallas_call(
        functools.partial(kernel, sizes),
        out_shape=(jax.ShapeDtypeStruct((tiers, rows, cols), F32), jax.ShapeDtypeStruct(theta.shape, F32)),
        in_specs=[hbm] * 7 + [pl.BlockSpec(memory_space=pltpu.SMEM)] + [hbm] * 3,
        out_specs=(vmem, vmem),
        scratch_shapes=[
            pltpu.VMEM((tiers, 2, taps), jnp.int32),
            pltpu.VMEM((tiers, 2, taps), F32),
            pltpu.VMEM((tiers, rows, cols), jnp.int32),
            *[pltpu.VMEM(size, F32) for size in scratch],
            dma((14,)), dma((8, tiers)), dma((8, tiers)), dma((8,)), dma((8,)), dma((tiers,)), dma((tiers,)),
        ],
        compiler_params=pltpu.CompilerParams(
            collective_id=0, has_side_effects=True, vmem_limit_bytes=56 * 2**20
        ),
        name="electrothermal",
    )(
        tap_index.reshape(tiers, 2, taps), tap_current.reshape(tiers, 2, taps), density, pad_cond, row_cond, col_cond,
        material, leak_rates, theta, kappa, invc,
    )


def solution(mesh):
    sizes = tuple(mesh.shape[name] for name in ("gx", "gy", "gz"))
    mesh_field = P("gz", "gx", "gy")
    tap = P("gz", "gx", "gy", None)
    block = P(None, "gx", ("gy", "gz"))
    return jax.shard_map(
        functools.partial(shards, sizes),
        mesh=mesh,
        in_specs=(mesh_field, tap, tap, mesh_field, mesh_field, mesh_field, mesh_field, P(), block, block, block),
        out_specs=(mesh_field, block),
        check_vma=False,
    )
```

time: 73 us -> 52 us (0.71)
  the two profiles are of different devices: /device:TPU:8 before, /device:TPU:1 now
where the time goes in v2:
time: 52 us; the launch traced here: 51.9 us
  Pallas kernels  47.3 us (91%)
  local copies, waits for them, and re-layouts  3.98 us (8%)
  between operations  0.64 us (1%)
    pallas_call x1, Pallas kernels, shards(): pl.pallas_call(functools.partial(kernel, sizes), out_shape=(jax.ShapeDtyp...  47.3 us
    unnamed x2, local copies, waits for them, and re-layouts  3.98 us

profile of v2, /device:TPU:1, one launch (start us, length us, event | category | flops | bytes accessed | tf_op | source)
XLA Modules:
  0.0 51.9 jit_solution(15056033064565352471)
XLA Ops:
  0.6 47.3 %electrothermal.1 = (f32[4,64,256]{2,1,0:T(8,128)}, f32[32,64,128]{2,1,0:T(8,128)}) custom-call(s32[4,2,128]{2,1,0:T(2,128)} %bitcast.2, f32[4,2,128]{2,1,0:T(2,128)} %bitcast.3, f32[4,64,256]{2,1,0:T(8,128)} %dens_hbm.1, f32[4,64,256]{2,1,0:T(8,128)} %pad_hbm.1, f32[4,64,256]{2,1,0:T(8,128)} %row_hbm.1, f32[4,64,256]{2,1,0:T(8,128)} %col_hbm.1, ...), custom_call_target="tpu_custom_call" | custom-call | tf_op jit(solution)/shard_map/electrothermal/pallas_call | solution.py:486
  47.9 1.7 %copy.15 = f32[4,64,256]{2,1,0:T(8,128)} copy(f32[4,64,256]{2,1,0:T(8,128)} %get-tuple-element.4) | data formatting | bytes 524288
  49.6 2.3 %copy.16 = f32[32,64,128]{2,1,0:T(8,128)} copy(f32[32,64,128]{2,1,0:T(8,128)} %get-tuple-element.5) | data formatting | bytes 2097152

commit v3 on v2

--- a/solution.py
+++ b/solution.py
@@ -52,11 +52,11 @@
 
 def kernel(
     sizes,
-    tidx_hbm, tcur_hbm, dens_hbm, pad_hbm, row_hbm, col_hbm, mat_hbm, rates, theta_hbm, kappa_hbm, invc_hbm,
+    tidx_hbm, tcur_hbm, dens_hbm, pad_hbm, row_hbm, col_hbm, mat_hbm, rates_hbm, theta_hbm, kappa_hbm, invc_hbm,
     drop_out, temp_out,
-    tidx, tcur, mat, ext, row_send, row_recv, col_send, xr, yr, coef, raw, ub, nat, unat,
+    tidx, tcur, mat, rates, ext, row_send, row_recv, col_send, xr, yr, coef, raw, ub, nat, unat,
     field, trow_send, trow, tcol_send, tx, ty, edge, heat_send, heat,
-    temp, cap, lx, ly, lz, snat, stemp, scap, slx, sly, slz, sground, sheat, mix, onat,
+    temp, east, west, aligned, cap, lx, ly, lw, lz, snat, stemp, scap, slx, sly, slz, sground, sheat, mix, begin, onat,
     isem, ssem, rsem, tssem, trsem, pssem, prsem,
 ):
     nx, ny, nz = sizes
@@ -73,6 +73,7 @@
                 ref.at[:, :, pl.ds(tile * 128, 128)], ext.at[a, :, tile, pl.ds(TOP, rows)], isem.at[len(loads)]
             ))
     loads.append(pltpu.make_async_copy(mat_hbm, mat, isem.at[len(loads)]))
+    loads.append(pltpu.make_async_copy(rates_hbm, rates, isem.at[len(loads)]))
     heat_loads = [
         pltpu.make_async_copy(ref, field.at[a, :, pl.ds(8, rows)], isem.at[len(loads) + a])
         for a, ref in enumerate((theta_hbm, kappa_hbm, invc_hbm))
@@ -235,7 +236,7 @@
     lane_rows = iota((rows + 2 * TOP, 128), 1)
     half = iota((8, 128), 1) < 64
 
-    def tier(t, carry):
+    def halos(t, i):
         for d in range(8):
             mesh_copy(d, t).wait_recv()
         for a in range(5):
@@ -256,63 +257,73 @@
         def fetch(a, start):
             return jnp.concatenate([ext[a, t, tile, pl.ds(start, 8, stride=V), :] for tile in range(3)], 1)
 
-        roots, gxm = [], fetch(GXP, TOP - HALO - 1)
+        gxm = fetch(GXP, TOP - HALO - 1)
         for v in range(V):
             src, pd, gxp, gyp, leak = [fetch(a, TOP - HALO + v) for a in range(5)]
             r = jnp.where(inside, inverse_root(pd + gxp + gxm + gyp + roll(gyp, 1, 1)), 0.0)
             gxm = gxp
-            for i, x in enumerate((pd, gxp, gyp, leak, r)):
-                raw[i, v] = x
-            coef[0, v] = src * r
-            coef[2, v] = gyp * r * roll(r, -1, 1)
+            for j, x in enumerate((pd, gxp, gyp, leak, r)):
+                raw[i, j, v] = x
+            coef[i, 0, v] = src * r
+            coef[i, 2, v] = gyp * r * roll(r, -1, 1)
         for v in range(V):
-            after = raw[4, v + 1] if v < V - 1 else roll(raw[4, 0], -1, 0)
-            coef[1, v] = raw[1, v] * raw[4, v] * after
-        coef[1, V] = roll(coef[1, V - 1], 1, 0)
-
-        def sweep(source_of, out):
-            here = source_of(0)
-            before, link_before = roll(source_of(V - 1), 1, 0), coef[1, V]
-            for v in range(V):
-                after = source_of(v + 1) if v < V - 1 else roll(source_of(0), -1, 0)
-                link, side = coef[1, v], coef[2, v]
-                flow = link * after + link_before * before
-                flow = flow + (side * roll(here, -1, 1) + roll(side * here, 1, 1))
-                ub[out, v] = coef[0, v] + flow
-                before, here, link_before = here, after, link
-
-        sweep(lambda v: coef[0, v], 0)
-
-        def two_sweeps(count, held):
-            sweep(lambda v: ub[0, v], 1)
-            sweep(lambda v: ub[1, v], 0)
-            return held
-
-        lax.fori_loop(0, (SWEEPS - 2) // 2, two_sweeps, 0)
-        here = first = ub[0, 0] * raw[4, 0]
+            after = raw[i, 4, v + 1] if v < V - 1 else roll(raw[i, 4, 0], -1, 0)
+            coef[i, 1, v] = raw[i, 1, v] * raw[i, 4, v] * after
+        coef[i, 1, V] = roll(coef[i, 1, V - 1], 1, 0)
+
+    def sweep(source_of, i, out):
+        here = source_of(0)
+        before, link_before = roll(source_of(V - 1), 1, 0), coef[i, 1, V]
         for v in range(V):
-            after = ub[0, v + 1] * raw[4, v + 1] if v < V - 1 else roll(first, -1, 0)
+            after = source_of(v + 1) if v < V - 1 else roll(source_of(0), -1, 0)
+            link, side = coef[i, 1, v], coef[i, 2, v]
+            flow = link * after + link_before * before
+            flow = flow + (side * roll(here, -1, 1) + roll(side * here, 1, 1))
+            ub[i, out, v] = coef[i, 0, v] + flow
+            before, here, link_before = here, after, link
+
+    def power_of(t, i):
+        here = first = ub[i, 0, 0] * raw[i, 4, 0]
+        for v in range(V):
+            after = ub[i, 0, v + 1] * raw[i, 4, v + 1] if v < V - 1 else roll(first, -1, 0)
             across, along = after - here, roll(here, -1, 1) - here
-            power = raw[0, v] * here * here + raw[1, v] * across * across + raw[2, v] * along * along
-            power = power + raw[3, v] * jnp.exp(-here)
+            power = raw[i, 0, v] * here * here + raw[i, 1, v] * across * across + raw[i, 2, v] * along * along
+            power = power + raw[i, 3, v] * jnp.exp(-here)
             at = pl.ds(TOP - HALO + v, 8, stride=V)
             for tile in range(3):
-                nat[tile, at, :] = power[:, tile * 128 : tile * 128 + 128]
+                nat[i, tile, at, :] = power[:, tile * 128 : tile * 128 + 128]
                 if tile < 2:
-                    unat[tile, at, :] = here[:, tile * 128 : tile * 128 + 128]
+                    unat[i, tile, at, :] = here[:, tile * 128 : tile * 128 + 128]
             here = after
 
         for v in range(W):
             at = pl.ds(TOP - 4 + v, 8, stride=W)
             for z, into in ((1 - gz, heat_send.at[t]), (gz, heat.at[gz * tiers + t])):
-                into[0, v] = nat[z, at, :]
-                into[1, v] = jnp.where(half, nat[1 + z, at, :], nat[2 - 2 * z, at, :])
+                into[0, v] = nat[i, z, at, :]
+                into[1, v] = jnp.where(half, nat[i, 1 + z, at, :], nat[i, 2 - 2 * z, at, :])
         power_copy(t, gz).start()
         for tile in range(2):
-            drop_out[t, :, tile * 128 : tile * 128 + 128] = unat[tile, TOP : TOP + rows, :]
+            drop_out[t, :, tile * 128 : tile * 128 + 128] = unat[i, tile, TOP : TOP + rows, :]
+
+    def pair(p, carry):
+        def each(work):
+            lax.fori_loop(0, 2, lambda i, held: (work(2 * p + i, i), held)[1], 0)
+
+        each(halos)
+        for i in range(2):
+            sweep(lambda v: coef[i, 0, v], i, 0)
+
+        def two_sweeps(count, held):
+            for here in range(2):
+                for i in range(2):
+                    sweep(lambda v: ub[i, here, v], i, 1 - here)
+            return held
+
+        lax.fori_loop(0, (SWEEPS - 2) // 2, two_sweeps, 0)
+        each(power_of)
         return carry
 
-    lax.fori_loop(0, tiers, tier, 0)
+    lax.fori_loop(0, tiers // 2, pair, 0)
 
     for d in range(8):
         heat_copy(d).wait_recv()
@@ -373,21 +384,32 @@
             link = harmonic(k[h], over[h])
             slz[s] = jnp.where(lane < 120, link, 0.0) if h else link
             if side:
-                mix[h] = k[h]
+                mix[h] = jnp.where((lane & 7) == 3, sly[2 * h], k[h])
+                begin[h] = jnp.where((lane & 7) == 3, stemp[2 * h], stemp[s])
+
+    def beside(x, beyond):
+        right = roll(jnp.where(lane == 0, beyond, x), -1, 2)
+        left = roll(jnp.where(lane == 127, beyond, x), 1, 2)
+        return right, left
 
     def links(layer, k):
-        temp[layer] = strided(field.at[0, layer])
+        x = strided(field.at[0, layer])
+        temp[0, layer] = x
+        east[0, layer], west[0, layer] = beside(x, align(begin[layer // 16], layer))
         cap[layer] = strided(field.at[2, layer])
         over = strided(field.at[1, jnp.minimum(layer + 1, layers - 1)])
-        beside = roll(jnp.where(lane == 0, align(mix[layer // 16], layer), k), -1, 2)
+        beyond = align(mix[layer // 16], layer)
+        right = harmonic(k, roll(jnp.where(lane == 0, beyond, k), -1, 2))
+        right = jnp.where(no_col, 0.0, right)
         lx[layer] = jnp.where(no_row, 0.0, harmonic(k, next_row(k)))
-        ly[layer] = jnp.where(no_col, 0.0, harmonic(k, beside))
+        ly[layer] = right
+        lw[layer] = roll(jnp.where(lane == 127, beyond, right), 1, 2)
         lz[layer + 1] = jnp.where(layer == layers - 1, 0.0, harmonic(k, over))
         return over
 
     ground = strided(field.at[1, 0])
     lz[0] = ground
-    lax.fori_loop(0, layers, links, ground)
+    lax.fori_loop(0, layers, links, ground, unroll=4)
 
     for t in range(tiers):
         power_copy(t, 1 - gz).wait()
@@ -402,7 +424,7 @@
         sheat[2 * h] = left
         sheat[2 * h + 1] = right
 
-    def step(count, carry):
+    def strips():
         for side in range(2):
             old = [stemp[side], stemp[2 + side]]
             over = upper(*old)
@@ -417,33 +439,51 @@
                 fx = slx[s] * (next_row(here) - here)
                 fy = sly[s] * (roll(here, -1, 2) - here)
                 flow = (fx - last_row(fx)) + (fy - roll(fy, 1, 2)) + (rise[h] - under[h]) + sheat[s]
-                stemp[s] = here + scap[s] * flow
-                mix[h] = jnp.where((lane & 7) == 3, mix[h], here) if side else fy
-
-        def per_tier(tier, below):
+                after = here + scap[s] * flow
+                stemp[s] = after
+                mix[h] = jnp.where((lane & 7) == 3, mix[h], after) if side else after
+
+    def shift(layer, into):
+        return beside(temp[into, layer], aligned[layer])
+
+    for count in range(STEPS):
+        now, then, more = count % 2, 1 - count % 2, count < STEPS - 1
+        if more:
+            strips()
+        if count:
+            for layer in range(layers - 4, layers):
+                east[now, layer], west[now, layer] = shift(layer, now)
+
+        def group(g, below, now=now, then=then, more=more):
+            base = 4 * g
+            if more:
+                prior = 4 * jnp.maximum(g - 1, 0)
+                shifted = [shift(prior + part, then) for part in range(4)]
+            fresh = []
+            here = temp[now, base]
             for part in range(4):
-                layer = tier * 4 + part
-                here = temp[layer]
-                beyond = align(mix[tier // 4], layer)
+                layer = base + part
+                over = temp[now, layer + 1 if part < 3 else jnp.minimum(layer + 1, layers - 1)]
                 fx = lx[layer] * (next_row(here) - here)
-                fy = ly[layer] * (roll(jnp.where(lane == 0, beyond, here), -1, 2) - here)
-                fz = lz[layer + 1] * (temp[jnp.minimum(layer + 1, layers - 1)] - here)
-                before = roll(jnp.where(lane == 127, beyond, fy), 1, 2)
-                flow = (fx - last_row(fx)) + (fy - before) + (fz - below)
+                fz = lz[layer + 1] * (over - here)
+                flow = ly[layer] * (east[now, layer] - here) + lw[layer] * (west[now, layer] - here)
+                flow = flow + (fx - last_row(fx)) + (fz - below)
                 if part == 0:
-                    flow = flow + heat[tier, 0]
-                temp[layer] = here + cap[layer] * flow
-                below = fz
+                    flow = flow + heat[g, 0]
+                fresh.append(here + cap[layer] * flow)
+                here, below = over, fz
+            for part in range(4):
+                temp[then, base + part] = fresh[part]
+                if more:
+                    east[then, prior + part], west[then, prior + part] = shifted[part]
+                    aligned[base + part] = align(mix[g // 4], base + part)
             return below
 
-        lax.fori_loop(0, layers // 4, per_tier, lz[0] * temp[0])
-        return carry
-
-    lax.fori_loop(0, STEPS, step, 0)
+        lax.fori_loop(0, layers // 4, group, lz[0] * temp[now, 0])
 
     def result(layer, carry):
         for v in range(W):
-            onat[layer, pl.ds(4 + v, 8, stride=W), :] = temp[layer, v]
+            onat[layer, pl.ds(4 + v, 8, stride=W), :] = temp[STEPS % 2, layer, v]
         temp_out[layer] = onat[layer, pl.ds(8, rows), :]
         return carry
 
@@ -462,7 +502,7 @@
 def shards(sizes, density, tap_index, tap_current, pad_cond, row_cond, col_cond, material, leak_rates, theta, kappa, invc):
     tiers, rows, cols = density.shape
     layers = theta.shape[0]
-    vmem, hbm = pl.BlockSpec(memory_space=pltpu.VMEM), pl.BlockSpec(memory_space=pl.ANY)
+    vmem, hbm = pl.BlockSpec(memory_space=pltpu.VMEM), pl.BlockSpec(memory_space=pltpu.HBM)
     tall, high = rows + 2 * TOP, rows + 16
     dma = pltpu.SemaphoreType.DMA
     taps = tap_index.shape[-1]
@@ -470,38 +510,42 @@
         (5, tiers, 3, tall, 128),
         (2, tiers, 88, cols), (2, tiers, 88, cols), (2, tiers, rows, 128),
         (tiers, tall, 128), (tiers, tall, 128),
-        (3, V + 1, 8, 384), (5, V, 8, 384), (2, V, 8, 384),
-        (3, tall, 128), (2, tall, 128),
+        (2, 3, V + 1, 8, 384), (2, 5, V, 8, 384), (2, 2, V, 8, 384),
+        (2, 3, tall, 128), (2, 2, tall, 128),
         (3, layers, high, 128),
         (2, 3, 16, 8, 128), (2, 3, 16, 8, 128),
         (2, 3, rows, 128), (3, high, 128), (3, high, 128), (3, 2, high, 128),
         (tiers, 2, W, 8, 128), (2 * tiers, 2, W, 8, 128),
+        (2, layers, W, 8, 128), (2, layers, W, 8, 128), (2, layers, W, 8, 128),
         (layers, W, 8, 128), (layers, W, 8, 128),
-        (layers, W, 8, 128), (layers, W, 8, 128), (layers + 1, W, 8, 128),
+        (layers, W, 8, 128), (layers, W, 8, 128), (layers, W, 8, 128), (layers + 1, W, 8, 128),
         (3, 4, high, 128),
         (4, W, 8, 128), (4, W, 8, 128), (4, W, 8, 128), (4, W, 8, 128), (4, W, 8, 128),
-        (2, W, 8, 128), (4, W, 8, 128), (2, W, 8, 128),
+        (2, W, 8, 128), (4, W, 8, 128), (2, W, 8, 128), (2, W, 8, 128),
         (layers, high, 128),
     ]
     return pl.pallas_call(
         functools.partial(kernel, sizes),
         out_shape=(jax.ShapeDtypeStruct((tiers, rows, cols), F32), jax.ShapeDtypeStruct(theta.shape, F32)),
-        in_specs=[hbm] * 7 + [pl.BlockSpec(memory_space=pltpu.SMEM)] + [hbm] * 3,
+        in_specs=[hbm] * 11,
         out_specs=(vmem, vmem),
         scratch_shapes=[
             pltpu.VMEM((tiers, 2, taps), jnp.int32),
             pltpu.VMEM((tiers, 2, taps), F32),
             pltpu.VMEM((tiers, rows, cols), jnp.int32),
+            pltpu.SMEM((MATERIALS,), F32),
             *[pltpu.VMEM(size, F32) for size in scratch],
-            dma((14,)), dma((8, tiers)), dma((8, tiers)), dma((8,)), dma((8,)), dma((tiers,)), dma((tiers,)),
+            dma((15,)), dma((8, tiers)), dma((8, tiers)), dma((8,)), dma((8,)), dma((tiers,)), dma((tiers,)),
         ],
         compiler_params=pltpu.CompilerParams(
-            collective_id=0, has_side_effects=True, vmem_limit_bytes=56 * 2**20
+            collective_id=0, has_side_effects=True, vmem_limit_bytes=34 * 2**20
         ),
         name="electrothermal",
     )(
-        tap_index.reshape(tiers, 2, taps), tap_current.reshape(tiers, 2, taps), density, pad_cond, row_cond, col_cond,
-        material, leak_rates, theta, kappa, invc,
+        *[pltpu.with_memory_space_constraint(x, pltpu.HBM) for x in (
+            tap_index.reshape(tiers, 2, taps), tap_current.reshape(tiers, 2, taps), density, pad_cond, row_cond,
+            col_cond, material, leak_rates, theta, kappa, invc,
+        )],
     )
 
 

time: 52 us -> 43.6 us (0.84)
  Pallas kernels: 47.3 us -> 41.2 us
  local copies, waits for them, and re-layouts: 3.98 us -> 1.67 us
    pallas_call x1, Pallas kernels: 47.3 us -> 41.2 us  [shards(): pl.pallas_call(functools.partial(kernel, sizes), out_shape=(jax.ShapeDtyp...]
    unnamed x2, local copies, waits for them, and re-layouts: 3.98 us -> 1.67 us
where the time goes in v3:
time: 43.6 us; the launch traced here: 43.5 us
  Pallas kernels  41.2 us (94%)
  local copies, waits for them, and re-layouts  1.67 us (4%)
  between operations  0.64 us (1%)
    pallas_call x1, Pallas kernels, shards(): pl.pallas_call(functools.partial(kernel, sizes), out_shape=(jax.ShapeDtyp...  41.2 us
    unnamed x2, local copies, waits for them, and re-layouts  1.67 us

profile of v3, /device:TPU:1, one launch (start us, length us, event | category | flops | bytes accessed | tf_op | source)
XLA Modules:
  0.0 43.5 jit_solution(16796753496323980444)
XLA Ops:
  0.6 41.2 %electrothermal.1 = (f32[4,64,256]{2,1,0:T(8,128)S(1)}, f32[32,64,128]{2,1,0:T(8,128)S(1)}) custom-call(s32[4,2,128]{2,1,0:T(2,128)} %bitcast.2, f32[4,2,128]{2,1,0:T(2,128)} %bitcast.3, f32[4,64,256]{2,1,0:T(8,128)} %dens_hbm.1, f32[4,64,256]{2,1,0:T(8,128)} %pad_hbm.1, f32[4,64,256]{2,1,0:T(8,128)} %row_hbm.1, f32[4,64,256]{2,1,0:T(8,128)} %col_hbm.1, ...), custom_call_target="tpu_custom_call" | custom-call | tf_op jit(solution)/shard_map/electrothermal/pallas_call | solution.py:527
  41.8 0.7 %copy.15 = f32[4,64,256]{2,1,0:T(8,128)} copy(f32[4,64,256]{2,1,0:T(8,128)S(1)} %get-tuple-element.4) | data formatting | bytes 524288
  42.5 1.0 %copy.16 = f32[32,64,128]{2,1,0:T(8,128)} copy(f32[32,64,128]{2,1,0:T(8,128)S(1)} %get-tuple-element.5) | data formatting | bytes 2097152

commit v4 on v3

--- a/solution.py
+++ b/solution.py
@@ -13,6 +13,7 @@
 STEPS = 4
 MATERIALS = 4
 HALO = 20
+DEEP = 19
 PITCH = 24
 TOP = 24
 V = 13
@@ -56,7 +57,7 @@
     drop_out, temp_out,
     tidx, tcur, mat, rates, ext, row_send, row_recv, col_send, xr, yr, coef, raw, ub, nat, unat,
     field, trow_send, trow, tcol_send, tx, ty, edge, heat_send, heat,
-    temp, east, west, aligned, cap, lx, ly, lw, lz, snat, stemp, scap, slx, sly, slz, sground, sheat, mix, begin, onat,
+    temp_a, temp_b, east_a, east_b, west_a, west_b, aligned, cap, lx, ly, lw, lz, snat, stemp, scap, slx, sly, slz, sground, sheat, mix, begin, onat,
     isem, ssem, rsem, tssem, trsem, pssem, prsem,
 ):
     nx, ny, nz = sizes
@@ -78,7 +79,7 @@
         pltpu.make_async_copy(ref, field.at[a, :, pl.ds(8, rows)], isem.at[len(loads) + a])
         for a, ref in enumerate((theta_hbm, kappa_hbm, invc_hbm))
     ]
-    for load in loads + heat_loads:
+    for load in loads:
         load.start()
 
     def mesh_to(d):
@@ -98,7 +99,8 @@
     for d in range(2, 8):
         pl.semaphore_signal(barrier, inc=1, device_id=heat_to(d), device_id_type=MESH)
 
-    def mesh_copy(d, t):
+    def mesh_copy(d, p):
+        t = pl.ds(2 * p, 2)
         top, bottom = pl.ds(0, TOP), pl.ds(rows - TOP, TOP)
         if d < 2:
             src, dst = row_send.at[d, t], row_recv.at[d, t]
@@ -115,7 +117,7 @@
         else:
             src, dst = col_send.at[1, t, bottom], yr.at[t, pl.ds(0, TOP)]
         return pltpu.make_async_remote_copy(
-            src_ref=src, dst_ref=dst, send_sem=ssem.at[d, t], recv_sem=rsem.at[d, t],
+            src_ref=src, dst_ref=dst, send_sem=ssem.at[d, p], recv_sem=rsem.at[d, p],
             device_id=mesh_to(d), device_id_type=MESH,
         )
 
@@ -178,29 +180,35 @@
             packed = jnp.zeros((rows, 128), F32)
             part = pl.ds(tile * 128, 128)
             for a, values in enumerate((source, pad, gxp, gyp, leak)):
+                deep = DEEP if a < LEAK else 3
+                at = a * DEEP
+                row_send[0, t, at : at + deep, part] = values[:deep]
+                row_send[1, t, at : at + deep, part] = values[rows - deep :]
                 size = HALO if a < LEAK else 4
-                at = a * HALO if a < LEAK else LEAK * HALO
-                row_send[0, t, at : at + size, part] = values[:size]
-                row_send[1, t, at : at + size, part] = values[rows - size :]
                 mine = (lane >= a * PITCH) & (lane < a * PITCH + size)
                 packed = jnp.where(mine, roll(values, a * PITCH + (size if tile else 0), 1), packed)
-            row_send[0, t, 84:88, part] = jnp.zeros((4, 128), F32)
-            row_send[1, t, 84:88, part] = jnp.zeros((4, 128), F32)
+            row_send[0, t, 79:80, part] = jnp.zeros((1, 128), F32)
+            row_send[1, t, 79:80, part] = jnp.zeros((1, 128), F32)
             col_send[tile, t] = packed
 
     def first_tiers(t, carry):
         prepare(t)
 
-        @pl.when(t == 0)
+        @pl.when(t == 1)
         def _():
             pl.semaphore_wait(barrier, 14)
 
-        for d in range(8):
-            mesh_copy(d, t).start()
+        @pl.when(lax.rem(t, 2) == 1)
+        def _():
+            for d in (4, 5, 6, 7, 0, 1, 2, 3):
+                mesh_copy(d, t // 2).start()
+
         return carry
 
     for load in loads:
         load.wait()
+    for load in heat_loads:
+        load.start()
     lax.fori_loop(0, tiers, first_tiers, 0)
 
     lane_tall = iota((rows, 128), 1)
@@ -228,28 +236,27 @@
         return carry
 
     lax.fori_loop(0, 3, gather, 0)
+
     for d in range(8):
         heat_copy(d).start()
 
     lane_ext = iota((8, 384), 1)
     inside = (lane_ext < cols + HALO) | (lane_ext >= 384 - HALO)
     lane_rows = iota((rows + 2 * TOP, 128), 1)
-    half = iota((8, 128), 1) < 64
+    lane_one = iota((8, 128), 1)
+    half = lane_one < 64
 
     def halos(t, i):
-        for d in range(8):
-            mesh_copy(d, t).wait_recv()
         for a in range(5):
-            size = HALO if a < LEAK else 4
-            at = a * HALO if a < LEAK else LEAK * HALO
+            size, deep = (HALO, DEEP) if a < LEAK else (4, 3)
+            at = a * DEEP
+            outside = jnp.full((TOP, 128), 1.0 if a == PAD else 0.0, F32)
             for tile in range(2):
                 part = pl.ds(tile * 128, 128)
-                ext[a, t, tile, 0:8, :] = jnp.zeros((8, 128), F32)
-                ext[a, t, tile, TOP - size : TOP, :] = row_recv[1, t, at : at + size, part]
-                ext[a, t, tile, TOP + rows : TOP + rows + size, :] = row_recv[0, t, at : at + size, part]
-                if a == LEAK:
-                    ext[a, t, tile, 8 : TOP - size, :] = jnp.zeros((TOP - size - 8, 128), F32)
-                    ext[a, t, tile, TOP + rows + size :, :] = jnp.zeros((TOP - size, 128), F32)
+                ext[a, t, tile, 0:TOP, :] = outside
+                ext[a, t, tile, TOP - deep : TOP, :] = row_recv[1, t, at : at + deep, part]
+                ext[a, t, tile, TOP + rows :, :] = outside
+                ext[a, t, tile, TOP + rows : TOP + rows + deep, :] = row_recv[0, t, at : at + deep, part]
             ext[a, t, 2] = jnp.where(
                 lane_rows < 64, roll(xr[t], -a * PITCH, 1), roll(yr[t], 128 - size - a * PITCH, 1)
             )
@@ -296,11 +303,14 @@
                     unat[i, tile, at, :] = here[:, tile * 128 : tile * 128 + 128]
             here = after
 
-        for v in range(W):
-            at = pl.ds(TOP - 4 + v, 8, stride=W)
-            for z, into in ((1 - gz, heat_send.at[t]), (gz, heat.at[gz * tiers + t])):
-                into[0, v] = nat[i, z, at, :]
-                into[1, v] = jnp.where(half, nat[i, 1 + z, at, :], nat[i, 2 - 2 * z, at, :])
+        for z, into in ((1 - gz, heat_send.at[t]), (gz, heat.at[gz * tiers + t])):
+            packed = jnp.zeros((8, 128), F32)
+            for v in range(W):
+                at = pl.ds(TOP - 4 + v, 8, stride=W)
+                into[v] = nat[i, z, at, :]
+                outer = jnp.where(half, nat[i, 1 + z, at, :], nat[i, 2 - 2 * z, at, :])
+                packed = jnp.where((lane_one >> 3) == v, roll(outer, 8 * v + 4, 1), packed)
+            into[W] = packed
         power_copy(t, gz).start()
         for tile in range(2):
             drop_out[t, :, tile * 128 : tile * 128 + 128] = unat[i, tile, TOP : TOP + rows, :]
@@ -309,6 +319,8 @@
         def each(work):
             lax.fori_loop(0, 2, lambda i, held: (work(2 * p + i, i), held)[1], 0)
 
+        for d in range(8):
+            mesh_copy(d, p).wait_recv()
         each(halos)
         for i in range(2):
             sweep(lambda v: coef[i, 0, v], i, 0)
@@ -392,13 +404,20 @@
         left = roll(jnp.where(lane == 127, beyond, x), 1, 2)
         return right, left
 
+    def bring(layer, carry):
+        aligned[layer] = align(begin[layer // 16], layer)
+        east_b[layer] = align(mix[layer // 16], layer)
+        return carry
+
+    lax.fori_loop(0, layers, bring, 0, unroll=4)
+
     def links(layer, k):
         x = strided(field.at[0, layer])
-        temp[0, layer] = x
-        east[0, layer], west[0, layer] = beside(x, align(begin[layer // 16], layer))
+        temp_a[layer] = x
+        east_a[layer], west_a[layer] = beside(x, aligned[layer])
         cap[layer] = strided(field.at[2, layer])
         over = strided(field.at[1, jnp.minimum(layer + 1, layers - 1)])
-        beyond = align(mix[layer // 16], layer)
+        beyond = east_b[layer]
         right = harmonic(k, roll(jnp.where(lane == 0, beyond, k), -1, 2))
         right = jnp.where(no_col, 0.0, right)
         lx[layer] = jnp.where(no_row, 0.0, harmonic(k, next_row(k)))
@@ -417,7 +436,8 @@
     for h in range(2):
         left = right = jnp.zeros(shape, F32)
         for t in range(4):
-            inner, outer = heat[h * 4 + t, 0], heat[h * 4 + t, 1]
+            inner, packed = heat[h * 4 + t, 0:W], heat[h * 4 + t, W]
+            outer = jnp.stack([roll(packed, -8 * v - 4, 1) for v in range(W)])
             mine = (lane >> 3) == 4 * t
             left = jnp.where(mine, roll(jnp.where(lane < 64, inner, outer), 32 * t + 4, 2), left)
             right = jnp.where(mine, roll(jnp.where(lane < 64, outer, inner), 32 * t + 4, 2), right)
@@ -443,60 +463,62 @@
                 stemp[s] = after
                 mix[h] = jnp.where((lane & 7) == 3, mix[h], after) if side else after
 
-    def shift(layer, into):
-        return beside(temp[into, layer], aligned[layer])
-
+    def shift(layer, state):
+        temp, east, west = state
+        east[layer], west[layer] = beside(temp[layer], aligned[layer])
+
+    states = ((temp_a, east_a, west_a), (temp_b, east_b, west_b))
     for count in range(STEPS):
-        now, then, more = count % 2, 1 - count % 2, count < STEPS - 1
+        now, then, more = states[count % 2], states[1 - count % 2], count < STEPS - 1
         if more:
             strips()
         if count:
             for layer in range(layers - 4, layers):
-                east[now, layer], west[now, layer] = shift(layer, now)
+                shift(layer, now)
 
         def group(g, below, now=now, then=then, more=more):
+            temp, east, west = now
             base = 4 * g
             if more:
-                prior = 4 * jnp.maximum(g - 1, 0)
-                shifted = [shift(prior + part, then) for part in range(4)]
-            fresh = []
-            here = temp[now, base]
+                for part in range(4):
+                    shift(4 * jnp.maximum(g - 1, 0) + part, then)
             for part in range(4):
                 layer = base + part
-                over = temp[now, layer + 1 if part < 3 else jnp.minimum(layer + 1, layers - 1)]
-                fx = lx[layer] * (next_row(here) - here)
-                fz = lz[layer + 1] * (over - here)
-                flow = ly[layer] * (east[now, layer] - here) + lw[layer] * (west[now, layer] - here)
-                flow = flow + (fx - last_row(fx)) + (fz - below)
-                if part == 0:
-                    flow = flow + heat[g, 0]
-                fresh.append(here + cap[layer] * flow)
-                here, below = over, fz
-            for part in range(4):
-                temp[then, base + part] = fresh[part]
+                over = layer + 1 if part < 3 else jnp.minimum(layer + 1, layers - 1)
+                fx_last = roll(lx[layer, W - 1] * (roll(temp[layer, 0], -1, 0) - temp[layer, W - 1]), 1, 0)
+                rise = []
+                for v in range(W):
+                    here = temp[layer, v]
+                    after = temp[layer, v + 1] if v < W - 1 else roll(temp[layer, 0], -1, 0)
+                    fx = lx[layer, v] * (after - here)
+                    fz = lz[layer + 1, v] * (temp[over, v] - here)
+                    flow = ly[layer, v] * (east[layer, v] - here) + lw[layer, v] * (west[layer, v] - here)
+                    flow = flow + (fx - fx_last) + (fz - below[v])
+                    if part == 0:
+                        flow = flow + heat[g, v]
+                    then[0][layer, v] = here + cap[layer, v] * flow
+                    fx_last = fx
+                    rise.append(fz)
+                below = tuple(rise)
                 if more:
-                    east[then, prior + part], west[then, prior + part] = shifted[part]
-                    aligned[base + part] = align(mix[g // 4], base + part)
+                    aligned[layer] = align(mix[g // 4], layer)
             return below
 
-        lax.fori_loop(0, layers // 4, group, lz[0] * temp[now, 0])
+        lax.fori_loop(0, layers // 4, group, tuple(lz[0, v] * now[0][0, v] for v in range(W)))
 
     def result(layer, carry):
         for v in range(W):
-            onat[layer, pl.ds(4 + v, 8, stride=W), :] = temp[STEPS % 2, layer, v]
+            onat[layer, pl.ds(4 + v, 8, stride=W), :] = states[STEPS % 2][0][layer, v]
         temp_out[layer] = onat[layer, pl.ds(8, rows), :]
         return carry
 
     lax.fori_loop(0, layers, result, 0, unroll=4)
 
-    def finish(t, carry):
-        for d in range(8):
-            mesh_copy(d, t).wait_send()
-        return carry
-
-    lax.fori_loop(0, tiers, finish, 0)
     for d in range(8):
         heat_copy(d).wait_send()
+    for p in range(tiers // 2):
+        for d in range(8):
+            mesh_copy(d, p).wait_send()
 
 
 def shards(sizes, density, tap_index, tap_current, pad_cond, row_cond, col_cond, material, leak_rates, theta, kappa, invc):
@@ -508,15 +530,15 @@
     taps = tap_index.shape[-1]
     scratch = [
         (5, tiers, 3, tall, 128),
-        (2, tiers, 88, cols), (2, tiers, 88, cols), (2, tiers, rows, 128),
+        (2, tiers, 80, cols), (2, tiers, 80, cols), (2, tiers, rows, 128),
         (tiers, tall, 128), (tiers, tall, 128),
         (2, 3, V + 1, 8, 384), (2, 5, V, 8, 384), (2, 2, V, 8, 384),
         (2, 3, tall, 128), (2, 2, tall, 128),
         (3, layers, high, 128),
         (2, 3, 16, 8, 128), (2, 3, 16, 8, 128),
         (2, 3, rows, 128), (3, high, 128), (3, high, 128), (3, 2, high, 128),
-        (tiers, 2, W, 8, 128), (2 * tiers, 2, W, 8, 128),
-        (2, layers, W, 8, 128), (2, layers, W, 8, 128), (2, layers, W, 8, 128),
+        (tiers, W + 1, 8, 128), (2 * tiers, W + 1, 8, 128),
+        *[(layers, W, 8, 128)] * 6,
         (layers, W, 8, 128), (layers, W, 8, 128),
         (layers, W, 8, 128), (layers, W, 8, 128), (layers, W, 8, 128), (layers + 1, W, 8, 128),
         (3, 4, high, 128),
@@ -535,7 +557,7 @@
             pltpu.VMEM((tiers, rows, cols), jnp.int32),
             pltpu.SMEM((MATERIALS,), F32),
             *[pltpu.VMEM(size, F32) for size in scratch],
-            dma((15,)), dma((8, tiers)), dma((8, tiers)), dma((8,)), dma((8,)), dma((tiers,)), dma((tiers,)),
+            dma((15,)), dma((8, tiers // 2)), dma((8, tiers // 2)), dma((8,)), dma((8,)), dma((tiers,)), dma((tiers,)),
         ],
         compiler_params=pltpu.CompilerParams(
             collective_id=0, has_side_effects=True, vmem_limit_bytes=34 * 2**20

time: 43.6 us -> 41.5 us (0.952)
  the two profiles are of different devices: /device:TPU:1 before, /device:TPU:8 now
where the time goes in v4:
time: 41.5 us; the launch traced here: 41.4 us
  Pallas kernels  39.1 us (94%)
  local copies, waits for them, and re-layouts  1.67 us (4%)
  between operations  0.64 us (2%)
    pallas_call x1, Pallas kernels, shards(): pl.pallas_call(functools.partial(kernel, sizes), out_shape=(jax.ShapeDtyp...  39.1 us
    unnamed x2, local copies, waits for them, and re-layouts  1.67 us

profile of v4, /device:TPU:8, one launch (start us, length us, event | category | flops | bytes accessed | tf_op | source)
XLA Modules:
  0.0 41.4 jit_solution(18130320251133950859)
XLA Ops:
  0.6 39.1 %electrothermal.1 = (f32[4,64,256]{2,1,0:T(8,128)S(1)}, f32[32,64,128]{2,1,0:T(8,128)S(1)}) custom-call(s32[4,2,128]{2,1,0:T(2,128)} %bitcast.2, f32[4,2,128]{2,1,0:T(2,128)} %bitcast.3, f32[4,64,256]{2,1,0:T(8,128)} %dens_hbm.1, f32[4,64,256]{2,1,0:T(8,128)} %pad_hbm.1, f32[4,64,256]{2,1,0:T(8,128)} %row_hbm.1, f32[4,64,256]{2,1,0:T(8,128)} %col_hbm.1, ...), custom_call_target="tpu_custom_call" | custom-call | tf_op jit(solution)/shard_map/electrothermal/pallas_call | solution.py:549
  39.7 0.7 %copy.15 = f32[4,64,256]{2,1,0:T(8,128)} copy(f32[4,64,256]{2,1,0:T(8,128)S(1)} %get-tuple-element.4) | data formatting | bytes 524288
  40.4 1.0 %copy.16 = f32[32,64,128]{2,1,0:T(8,128)} copy(f32[32,64,128]{2,1,0:T(8,128)S(1)} %get-tuple-element.5) | data formatting | bytes 2097152

commit v5 on v4

--- a/solution.py
+++ b/solution.py
@@ -79,8 +79,6 @@
         pltpu.make_async_copy(ref, field.at[a, :, pl.ds(8, rows)], isem.at[len(loads) + a])
         for a, ref in enumerate((theta_hbm, kappa_hbm, invc_hbm))
     ]
-    for load in loads:
-        load.start()
 
     def mesh_to(d):
         dx, dy = DIRS[d]
@@ -98,6 +96,8 @@
         pl.semaphore_signal(barrier, inc=1, device_id=mesh_to(d), device_id_type=MESH)
     for d in range(2, 8):
         pl.semaphore_signal(barrier, inc=1, device_id=heat_to(d), device_id_type=MESH)
+    for load in loads:
+        load.start()
 
     def mesh_copy(d, p):
         t = pl.ds(2 * p, 2)
@@ -198,10 +198,10 @@
         def _():
             pl.semaphore_wait(barrier, 14)
 
-        @pl.when(lax.rem(t, 2) == 1)
+        @pl.when(t == 1)
         def _():
             for d in (4, 5, 6, 7, 0, 1, 2, 3):
-                mesh_copy(d, t // 2).start()
+                mesh_copy(d, 0).start()
 
         return carry
 
@@ -238,6 +238,10 @@
     lax.fori_loop(0, 3, gather, 0)
 
     for d in range(8):
+        mesh_copy(d, 0).wait_send()
+    for d in (4, 5, 6, 7, 0, 1, 2, 3):
+        mesh_copy(d, 1).start()
+    for d in (4, 5, 6, 7, 2, 3, 0, 1):
         heat_copy(d).start()
 
     lane_ext = iota((8, 384), 1)
@@ -516,9 +520,8 @@
 
     for d in range(8):
         heat_copy(d).wait_send()
-    for p in range(tiers // 2):
-        for d in range(8):
-            mesh_copy(d, p).wait_send()
+    for d in range(8):
+        mesh_copy(d, 1).wait_send()
 
 
 def shards(sizes, density, tap_index, tap_current, pad_cond, row_cond, col_cond, material, leak_rates, theta, kappa, invc):

time: 41.5 us -> 41.3 us (level)
  no operation moved by 1% of the time
where the time goes in v5:
time: 41.3 us; the launch traced here: 41.2 us
  Pallas kernels  38.9 us (94%)
  local copies, waits for them, and re-layouts  1.67 us (4%)
  between operations  0.64 us (2%)
    pallas_call x1, Pallas kernels, shards(): pl.pallas_call(functools.partial(kernel, sizes), out_shape=(jax.ShapeDtyp...  38.9 us
    unnamed x2, local copies, waits for them, and re-layouts  1.67 us

profile of v5, /device:TPU:8, one launch (start us, length us, event | category | flops | bytes accessed | tf_op | source)
XLA Modules:
  0.0 41.2 jit_solution(9734945982853028096)
XLA Ops:
  0.6 38.9 %electrothermal.1 = (f32[4,64,256]{2,1,0:T(8,128)S(1)}, f32[32,64,128]{2,1,0:T(8,128)S(1)}) custom-call(s32[4,2,128]{2,1,0:T(2,128)} %bitcast.2, f32[4,2,128]{2,1,0:T(2,128)} %bitcast.3, f32[4,64,256]{2,1,0:T(8,128)} %dens_hbm.1, f32[4,64,256]{2,1,0:T(8,128)} %pad_hbm.1, f32[4,64,256]{2,1,0:T(8,128)} %row_hbm.1, f32[4,64,256]{2,1,0:T(8,128)} %col_hbm.1, ...), custom_call_target="tpu_custom_call" | custom-call | tf_op jit(solution)/shard_map/electrothermal/pallas_call | solution.py:552
  39.5 0.7 %copy.15 = f32[4,64,256]{2,1,0:T(8,128)} copy(f32[4,64,256]{2,1,0:T(8,128)S(1)} %get-tuple-element.4) | data formatting | bytes 524288
  40.2 1.0 %copy.16 = f32[32,64,128]{2,1,0:T(8,128)} copy(f32[32,64,128]{2,1,0:T(8,128)S(1)} %get-tuple-element.5) | data formatting | bytes 2097152

commit v6 on v5

--- a/solution.py
+++ b/solution.py
@@ -500,7 +500,10 @@
                     flow = flow + (fx - fx_last) + (fz - below[v])
                     if part == 0:
                         flow = flow + heat[g, v]
-                    then[0][layer, v] = here + cap[layer, v] * flow
+                    if more:
+                        then[0][layer, v] = here + cap[layer, v] * flow
+                    else:
+                        onat[layer, pl.ds(4 + v, 8, stride=W), :] = here + cap[layer, v] * flow
                     fx_last = fx
                     rise.append(fz)
                 below = tuple(rise)
@@ -511,8 +514,6 @@
         lax.fori_loop(0, layers // 4, group, tuple(lz[0, v] * now[0][0, v] for v in range(W)))
 
     def result(layer, carry):
-        for v in range(W):
-            onat[layer, pl.ds(4 + v, 8, stride=W), :] = states[STEPS % 2][0][layer, v]
         temp_out[layer] = onat[layer, pl.ds(8, rows), :]
         return carry
 

time: 41.3 us -> 41.2 us (level)
  no operation moved by 1% of the time
where the time goes in v6:
time: 41.2 us; the launch traced here: 41.1 us
  Pallas kernels  38.8 us (94%)
  local copies, waits for them, and re-layouts  1.67 us (4%)
  between operations  0.64 us (2%)
    pallas_call x1, Pallas kernels, shards(): pl.pallas_call(functools.partial(kernel, sizes), out_shape=(jax.ShapeDtyp...  38.8 us
    unnamed x2, local copies, waits for them, and re-layouts  1.67 us

profile of v6, /device:TPU:8, one launch (start us, length us, event | category | flops | bytes accessed | tf_op | source)
XLA Modules:
  0.0 41.1 jit_solution(10792932693901362881)
XLA Ops:
  0.6 38.8 %electrothermal.1 = (f32[4,64,256]{2,1,0:T(8,128)S(1)}, f32[32,64,128]{2,1,0:T(8,128)S(1)}) custom-call(s32[4,2,128]{2,1,0:T(2,128)} %bitcast.2, f32[4,2,128]{2,1,0:T(2,128)} %bitcast.3, f32[4,64,256]{2,1,0:T(8,128)} %dens_hbm.1, f32[4,64,256]{2,1,0:T(8,128)} %pad_hbm.1, f32[4,64,256]{2,1,0:T(8,128)} %row_hbm.1, f32[4,64,256]{2,1,0:T(8,128)} %col_hbm.1, ...), custom_call_target="tpu_custom_call" | custom-call | tf_op jit(solution)/shard_map/electrothermal/pallas_call | solution.py:553
  39.4 0.7 %copy.15 = f32[4,64,256]{2,1,0:T(8,128)} copy(f32[4,64,256]{2,1,0:T(8,128)S(1)} %get-tuple-element.4) | data formatting | bytes 524288
  40.1 1.0 %copy.16 = f32[32,64,128]{2,1,0:T(8,128)} copy(f32[32,64,128]{2,1,0:T(8,128)S(1)} %get-tuple-element.5) | data formatting | bytes 2097152
